TPU v7x, 256 devices: a whole 4x4x8 slice. The times are simulated.
256 devices in a mesh: leaf: 16 (over x_hi, z), blk: 4 (over x_lo, core), kv: 4 (over y).
Axes of the slice: x: 4 (x_hi: 2, x_lo: 2; x = x_hi * 2 + x_lo), y: 4, z: 8, core: 2. Of those that a mesh axis runs over, the one named last changes fastest.
Arguments:
- queries: bfloat16 [32768, 2560], P(('leaf', 'blk', 'kv')), parts along dimension 0, may hold values from -8 to 8
- keys: bfloat16 [131072, 512], P(('leaf', 'blk', 'kv')), parts along dimension 0, may hold values from -8 to 8
- values: bfloat16 [131072, 512], P(('leaf', 'blk', 'kv')), parts along dimension 0, may hold values from -6 to 6
- ancestry: int32 [256, 64], P('leaf'), parts along dimension 0, may hold values from 0 to 1, as said below
- leaf_tiles: int32 [256], P('leaf'), parts along dimension 0, may hold values from 1 to 63, as said below
Outputs:
- attended: bfloat16 [32768, 2560], P(('leaf', 'blk', 'kv')), parts along dimension 0
There are 16 independent parts, one for each index of `leaf`. A program takes and returns all parts, laid end to end along the dimension named above; each array names one. Nothing has to cross between parts.
Inputs may be any that keep to these rules, and one draw needn't show every extreme that they name: ancestry[a, t] is 1 exactly when key tile t is a strict ancestor of tile leaf_tiles[a] in the tree whose nodes are the key tiles; tile 0 is the root of the tree. `leaf_tiles`: strictly rising; the last entry is 63.
All inputs are finite; a program needn't handle non-finite values.
Results may differ from a plain program's by a relative error of at most 0.018.
Values may be sent and summed in bfloat16 or wider, within the bound.
No kernel may reach another device: no remote copies, remote signals or barrier semaphores. Data moves between devices by JAX's collectives and lax.ppermute only.
A program may use at most 256 MiB of HBM per device.

v0:
```python
import functools
import math

import jax
import jax.numpy as jnp
from jax import lax
from jax.experimental import pallas as pl
from jax.experimental.pallas import tpu as pltpu
from jax.sharding import PartitionSpec as P

TILE = 128
KV_HEADS = 4
GROUP = 5
DH = 128
WIDE = GROUP * DH
RING = 4
BLKS = 4
LOW = -1e30
SCALE = math.log2(math.e) / math.sqrt(DH)


def in_hbm(array):
    return pltpu.with_memory_space_constraint(array, pltpu.HBM)


def in_vmem(array):
    return pltpu.with_memory_space_constraint(array, pltpu.VMEM)


def pack_kernel(queries_ref, keys_ref, values_ref, across_ref, first_ref, third_ref, q_ref, sems):
    me = lax.axis_index("kv")
    rows = keys_ref.shape[0]
    copies = []

    def move(source, target):
        copies.append(pltpu.make_async_copy(source, target, sems.at[len(copies)]))
        copies[-1].start()

    for step, target, start in ((0, across_ref, 0), (2, across_ref, 2 * rows), (1, first_ref, 0), (3, third_ref, 0)):
        head = lax.rem(me + step, RING)
        narrow = pl.ds(pl.multiple_of(head * DH, DH), DH)
        move(keys_ref.at[:, narrow], target.at[pl.ds(start, rows)])
        move(values_ref.at[:, narrow], target.at[pl.ds(start + rows, rows)])
    for step, target, start in ((1, first_ref, 2 * rows), (3, third_ref, 2 * rows), (2, q_ref, 0)):
        head = lax.rem(me + step, RING)
        for g in range(GROUP):
            narrow = pl.ds(pl.multiple_of((head * GROUP + g) * DH, DH), DH)
            move(queries_ref.at[:, narrow], target.at[pl.ds(start + g * TILE, TILE)])
    for copy in copies:
        copy.wait()


def pack(queries, keys, values):
    rows = 2 * keys.shape[0]
    hbm = pl.BlockSpec(memory_space=pltpu.HBM)
    vmem = pl.BlockSpec(memory_space=pltpu.VMEM)
    lengths = (2 * rows, rows + WIDE, rows + WIDE, WIDE)
    return pl.pallas_call(
        pack_kernel,
        out_shape=[pltpu.VMEM((length, DH), jnp.bfloat16) for length in lengths],
        in_specs=[hbm] * 3,
        out_specs=[vmem] * len(lengths),
        scratch_shapes=[pltpu.SemaphoreType.DMA((2 * RING + 3 * GROUP,))],
        compiler_params=pltpu.CompilerParams(vmem_limit_bytes=4 * 1024 * 1024),
        name="pack",
    )(in_hbm(queries), in_hbm(keys), in_hbm(values))


def unpack_kernel(*refs):
    parts, out_ref, sems = refs[1:RING], refs[RING], refs[RING + 1]
    me = lax.axis_index("kv")
    copies = []
    for i in range(RING - 1):
        wide = pl.ds(pl.multiple_of(lax.rem(me + i + 1, RING) * WIDE, DH), WIDE)
        copies.append(pltpu.make_async_copy(parts[i], out_ref.at[:, wide], sems.at[i]))
    for copy in copies:
        copy.start()
    for copy in copies:
        copy.wait()


def unpack(whole, parts):
    hbm = pl.BlockSpec(memory_space=pltpu.HBM)
    vmem = pl.BlockSpec(memory_space=pltpu.VMEM)
    return pl.pallas_call(
        unpack_kernel,
        out_shape=pltpu.HBM((TILE, KV_HEADS * WIDE), jnp.bfloat16),
        in_specs=[hbm] + [vmem] * (RING - 1),
        out_specs=hbm,
        input_output_aliases={0: 0},
        scratch_shapes=[pltpu.SemaphoreType.DMA((RING - 1,))],
        compiler_params=pltpu.CompilerParams(vmem_limit_bytes=4 * 1024 * 1024),
        name="unpack",
    )(in_hbm(whole), *[in_vmem(part) for part in parts])


def attend_kernel(steps, last, parts, table_ref, queries_ref, *refs):
    passed = [step for step in steps if step]
    q_refs = dict(zip(passed, refs))
    refs = refs[len(passed) :]
    kv_refs, refs = refs[:parts], refs[parts:]
    if last:
        before, o_refs, refs = refs[:3], refs[3 : 3 + len(steps)], refs[3 + len(steps) :]
        held, own_queries, own_held, peaks, totals, sums, sems = refs
    else:
        peaks, totals, sums, held, own_queries, own_held, sems = refs
    me = lax.axis_index("kv")
    fetches = []
    if 0 in steps:
        q_refs[0] = own_queries
        for g in range(GROUP):
            narrow = pl.ds(pl.multiple_of((me * GROUP + g) * DH, DH), DH)
            fetches.append(
                pltpu.make_async_copy(queries_ref.at[:, narrow], own_queries.at[pl.ds(g * TILE, TILE)], sems.at[g])
            )
            fetches[-1].start()
    place, rows = 0, held.shape[1]
    for kv_ref in kv_refs:
        for i in range(kv_ref.shape[0] // rows):
            held[place] = kv_ref[i * rows : (i + 1) * rows]
            place += 1
    rows = rows // 2
    tiles_each = rows // TILE
    ahead = lax.broadcasted_iota(jnp.int32, (TILE, TILE), 0) > lax.broadcasted_iota(jnp.int32, (TILE, TILE), 1)
    ahead = jnp.concatenate([ahead] * GROUP, axis=1)
    for fetch in fetches:
        fetch.wait()

    def tiles_of(which, slots):
        found = []
        for slot in slots:
            row = pl.multiple_of((slot % tiles_each) * TILE, TILE)
            found.append(held[slot // tiles_each, pl.ds(row + which * rows, TILE), :])
        return jnp.concatenate(found, axis=0)

    def visit(step, slots, shown, own, carried):
        peak, total, summed = carried
        q_ref = q_refs[step]
        raw = lax.dot_general(
            tiles_of(0, slots),
            q_ref[q_ref.shape[0] - WIDE :],
            (((1,), (1,)), ((), ())),
            preferred_element_type=jnp.float32,
        )
        if own:
            raw = jnp.where(ahead, LOW, raw)
        raw = [raw[i * TILE : (i + 1) * TILE] for i in range(len(slots))]
        higher = peak
        for part, show in zip(raw, shown):
            higher = jnp.maximum(higher, jnp.where(show, jnp.max(part, axis=0, keepdims=True), LOW))
        shift = higher * SCALE
        kept = jnp.exp2(peak * SCALE - shift)
        weights = [jnp.exp2(part * SCALE - jnp.where(show, shift, -LOW)) for part, show in zip(raw, shown)]
        total = total * kept
        for part in weights:
            total = total + jnp.sum(part, axis=0, keepdims=True)
        update = lax.dot_general(
            tiles_of(1, slots),
            jnp.concatenate(weights, axis=0).astype(jnp.bfloat16),
            (((0,), (0,)), ((), ())),
            preferred_element_type=jnp.float32,
        )
        return (higher, total, summed * kept + update)

    for i, step in enumerate(steps):
        row = step + RING if last else step
        if last:
            carried = tuple(ref[step] for ref in before)
        else:
            carried = (
                jnp.full((1, WIDE), LOW, jnp.float32),
                jnp.zeros((1, WIDE), jnp.float32),
                jnp.zeros((DH, WIDE), jnp.float32),
            )
        carried = visit(step, [table_ref[row, 2]], [table_ref[row, 1] == 1], True, carried)
        for ref, value in zip((peaks, totals, sums), carried):
            ref[i] = value

    fulls = [table_ref[step + RING if last else step, 0] for step in steps]
    most = functools.reduce(jnp.maximum, fulls)

    def round_of(start, width, at, carry):
        for i, (step, full) in enumerate(zip(steps, fulls)):
            row = step + RING if last else step
            tiles = [start + width * at + place for place in range(width)]
            slots = [table_ref[row, 3 + tile] for tile in tiles]
            shown = [tile < full for tile in tiles]
            carried = visit(step, slots, shown, False, (peaks[i], totals[i], sums[i]))
            for ref, value in zip((peaks, totals, sums), carried):
                ref[i] = value
        return carry

    fours = (most + 1) // 4
    lax.fori_loop(0, fours, functools.partial(round_of, 0, 4), 0)
    lax.fori_loop(0, (most - 4 * fours + 1) // 2, functools.partial(round_of, 4 * fours, 2), 0)

    if last:
        for i, (step, o_ref) in enumerate(zip(steps, o_refs)):
            result = sums[i] / totals[i]
            target = o_ref if step else own_held
            for g in range(GROUP):
                target[:, g * DH : (g + 1) * DH] = result[:, g * TILE : (g + 1) * TILE].T.astype(jnp.bfloat16)
            if step == 0:
                wide = pl.ds(pl.multiple_of(me * WIDE, DH), WIDE)
                place_own = pltpu.make_async_copy(own_held, o_ref.at[:, wide], sems.at[GROUP])
                place_own.start()
                place_own.wait()


def attend(steps, table, queries, query_parts, kv_parts, state, cost):
    last = state is not None
    rows = 2 * TILE * 4
    blocks = sum(part.shape[0] // rows for part in kv_parts)
    vmem = pl.BlockSpec(memory_space=pltpu.VMEM)
    smem = pl.BlockSpec(memory_space=pltpu.SMEM)
    hbm = pl.BlockSpec(memory_space=pltpu.HBM)
    operands = [table, in_hbm(queries), *[query_parts[step] for step in steps if step], *kv_parts]
    operands += list(state) if last else []
    in_specs = [smem, hbm] + [vmem] * (len(operands) - 2)
    state_shapes = [pltpu.VMEM((len(steps), length, WIDE), jnp.float32) for length in (1, 1, DH)]
    if last:
        outs = [
            pltpu.VMEM((TILE, WIDE), jnp.bfloat16)
            if step
            else pltpu.HBM((TILE, KV_HEADS * WIDE), jnp.bfloat16)
            for step in steps
        ]
        out_specs = [vmem if step else hbm for step in steps]
    else:
        outs, out_specs = state_shapes, [vmem] * 3
    return pl.pallas_call(
        functools.partial(attend_kernel, steps, last, len(kv_parts)),
        out_shape=outs,
        in_specs=in_specs,
        out_specs=out_specs,
        scratch_shapes=[
            pltpu.VMEM((blocks, rows, DH), jnp.bfloat16),
            pltpu.VMEM((WIDE, DH), jnp.bfloat16),
            pltpu.VMEM((TILE, WIDE), jnp.bfloat16),
            *(state_shapes if last else []),
            pltpu.SemaphoreType.DMA((GROUP + 1,)),
        ],
        compiler_params=pltpu.CompilerParams(vmem_limit_bytes=12 * 1024 * 1024),
        cost_estimate=pl.CostEstimate(flops=0, bytes_accessed=cost, transcendentals=0),
        name="attend_last" if last else "attend_first",
    )(*operands)


def tables_kernel(ancestry_ref, leaf_tiles_ref, table_ref):
    me, blk = lax.axis_index("kv"), lax.axis_index("blk")
    tiles = ancestry_ref.shape[1]
    each = tiles // (BLKS * RING)
    query_tiles = [blk * RING + lax.rem(me - step + RING, RING) for step in range(RING)]

    def place_of(tile):
        owner = tile // each
        relative = (owner // RING) ^ blk
        turned = (me - owner) & (RING - 1)
        low, high = relative & 1, relative // 2
        late = jnp.where((turned == 2) | ((turned != 0) & (high == 1)), 1, 0)
        early_block = low * RING + jnp.where(turned == 0, high, 2 + turned // 2)
        late_block = low * 2 + jnp.where(turned == 2, RING + high, turned // 2)
        block = jnp.where(late == 1, late_block, early_block)
        return late, block * each + (tile & (each - 1))

    def visit(tile, counts):
        late, place = place_of(tile)
        later = []
        for step in range(RING):
            linked = ancestry_ref[query_tiles[step], tile]
            early_count, late_count = counts[2 * step : 2 * step + 2]
            table_ref[step + late * RING, 3 + jnp.where(late == 1, late_count, early_count)] = place
            later += [early_count + linked * (1 - late), late_count + linked * late]
        return tuple(later)

    def clear(at, carried):
        for row in range(2 * RING):
            table_ref[row, at] = 0
        return carried

    lax.fori_loop(0, table_ref.shape[1], clear, 0)
    counts = lax.fori_loop(0, tiles, visit, (jnp.int32(0),) * (2 * RING))
    for step in range(RING):
        late, place = place_of(leaf_tiles_ref[query_tiles[step]])
        for side in range(2):
            table_ref[step + side * RING, 0] = counts[2 * step + side]
            table_ref[step + side * RING, 1] = jnp.where(late == side, 1, 0)
            table_ref[step + side * RING, 2] = jnp.where(late == side, place, 0)


def chain_tables(ancestry, leaf_tiles):
    smem = pl.BlockSpec(memory_space=pltpu.SMEM)
    return pl.pallas_call(
        tables_kernel,
        out_shape=jax.ShapeDtypeStruct((2 * RING, ancestry.shape[1] + 8), jnp.int32),
        in_specs=[smem, smem],
        out_specs=smem,
        compiler_params=pltpu.CompilerParams(vmem_limit_bytes=1024 * 1024),
        cost_estimate=pl.CostEstimate(flops=0, bytes_accessed=10**8, transcendentals=0),
        name="tables",
    )(ancestry, leaf_tiles)


def turn(array, by):
    return lax.ppermute(array, "kv", [(i, (i + by) % RING) for i in range(RING)])


def across(array, bit):
    return lax.ppermute(array, "blk", [(i, i ^ bit) for i in range(BLKS)])


def on_device(queries, keys, values, ancestry, leaf_tiles):
    table = chain_tables(ancestry, leaf_tiles)
    sent_across, sent_first, sent_third, sent_queries = pack(queries, keys, values)
    block = 2 * keys.shape[0]

    got_across = across(sent_across, 2)
    got_first, got_third = turn(sent_first, 1), turn(sent_third, 3)
    got_queries = turn(sent_queries, 2)
    sent_across, got_across, got_first, got_third, got_queries, table = lax.optimization_barrier(
        (sent_across, got_across, got_first, got_third, got_queries, table)
    )
    query_parts = {1: got_first, 2: got_queries, 3: got_third}

    own_sides = jnp.concatenate([got_first[:block], got_third[:block]], axis=0)
    far_sides = across(own_sides, 2)
    got_last = turn(jnp.concatenate([sent_across[block:], got_across[block:]], axis=0), 2)
    here = jnp.concatenate([sent_across[:block], got_across[:block]], axis=0)
    swapped_here, near_sides = across(here, 1), across(own_sides, 1)
    parts = [here, own_sides, swapped_here, near_sides]
    state = attend((0, 1, 2, 3), table, queries, query_parts, parts, None, 10**8)
    far_sides, got_last, *state = lax.optimization_barrier((far_sides, got_last, *state))

    diagonal_sides, swapped_last = across(far_sides, 1), across(got_last, 1)
    parts = [far_sides, diagonal_sides, got_last, swapped_last]
    out_first, out_third = attend((1, 3), table, queries, query_parts, parts, state, 10**8)
    back_first, back_third = turn(out_first, -1), turn(out_third, -3)
    table, *state = lax.optimization_barrier((out_first, table, *state))[1:]
    out_second, whole = attend((2, 0), table, queries, query_parts, parts, state, 10**8)
    out_second, back_first, back_third = lax.optimization_barrier((out_second, back_first, back_third))
    return unpack(whole, [back_first, turn(out_second, -2), back_third])


def solution(mesh):
    in_specs = (
        P(("leaf", "blk", "kv"), None),
        P(("leaf", "blk", "kv"), None),
        P(("leaf", "blk", "kv"), None),
        P("leaf", None),
        P("leaf"),
    )
    out_specs = P(("leaf", "blk", "kv"), None)
    return jax.shard_map(
        on_device, mesh=mesh, in_specs=in_specs, out_specs=out_specs, check_vma=False
    )
```

profile of v0, /device:TPU:2, one launch (start us, length us, event | category | flops | bytes accessed | tf_op | source)
XLA Modules:
  0.0 62.0 jit_solution(6915875281088170999)
XLA Ops:
  0.0 1.6 %pack.1 = (bf16[2048,128]{1,0:T(8,128)(2,1)S(1)}, bf16[1664,128]{1,0:T(8,128)(2,1)S(1)}, bf16[1664,128]{1,0:T(8,128)(2,1)S(1)}, bf16[640,128]{1,0:T(8,128)(2,1)S(1)}) custom-call(bf16[128,2560]{1,0:T(8,128)(2,1)} %queries_ref.7, bf16[512,512]{1,0:T(8,128)(2,1)} %keys_ref.1, bf16[512,512]{1,0:T(8,128)(2,1)} %values_ref.1), custom_call_target="tpu_custom_call" | custom-call | tf_op jit(solution)/shard_map/pack/pallas_call | solution.py:58
  1.6 2.4 %collective-permute-start = (bf16[2048,128]{1,0:T(8,128)(2,1)S(1)}, bf16[2048,128]{1,0:T(8,128)(2,1)S(1)}, u32[]{:S(2)}, u32[]{:S(2)}) collective-permute-start(bf16[2048,128]{1,0:T(8,128)(2,1)S(1)} %get-tuple-element.41), channel_id=1, source_target_pairs={{0,8},{4,12},{8,0},{12,4},{1,9},{5,13},{9,1},{13,5},{2,10},{6,14},... | collective-permute-start | bytes 1572872 | tf_op jit(solution)/shard_map/ppermute | solution.py:309
  3.9 0.0 collective-permute-start.1
  4.0 3.2 %collective-permute-start.2 = (bf16[1664,128]{1,0:T(8,128)(2,1)S(1)}, bf16[1664,128]{1,0:T(8,128)(2,1)S(1)}, u32[]{:S(2)}, u32[]{:S(2)}) collective-permute-start(bf16[1664,128]{1,0:T(8,128)(2,1)S(1)} %get-tuple-element.36), channel_id=1, source_target_pairs={{0,3},{1,0},{2,1},{3,2},{4,7},{5,4},{6,5},{7,6},{8,11},{9,8},{10,9... | collective-permute-start | bytes 1277960 | tf_op jit(solution)/shard_map/ppermute | solution.py:305
  7.2 0.2 collective-permute-start.3
  7.4 5.6 %tables.1.table_ref = s32[8,72]{1,0:T(8,128)S(1)} custom-call(s32[16,64]{1,0:T(8,128)S(1)} %copy-done, s32[16]{0:T(128)S(1)} %copy-done.1), custom_call_target="tpu_custom_call" | custom-call | bytes 100000000 | tf_op jit(solution)/shard_map/tables/pallas_call | solution.py:293
  13.0 6.4 %collective-permute-done.3.refs_1_.refs_0_ = bf16[640,128]{1,0:T(8,128)(2,1)S(1)} collective-permute-done((bf16[640,128]{1,0:T(8,128)(2,1)S(1)}, bf16[640,128]{1,0:T(8,128)(2,1)S(1)}, u32[]{:S(2)}, u32[]{:S(2)}) %collective-permute-start.3) | collective-permute-done | bytes 163872 | tf_op jit(solution)/shard_map/ppermute | solution.py:305
  19.5 0.0 collective-permute-done.1.refs_0_
  19.5 0.0 collective-permute-done.2.refs_2_.refs_1_
  19.5 0.0 collective-permute-done
  19.5 0.1 fusion
  19.6 0.1 collective-permute-start.6
  19.8 0.6 collective-permute-start.7
  20.4 0.8 %collective-permute-start.5 = (bf16[2048,128]{1,0:T(8,128)(2,1)S(1)}, bf16[2048,128]{1,0:T(8,128)(2,1)S(1)}, u32[]{:S(2)}, u32[]{:S(2)}) collective-permute-start(bf16[2048,128]{1,0:T(8,128)(2,1)S(1)} %pad_maximum_fusion.1), channel_id=1, source_target_pairs={{0,2},{1,3},{2,0},{3,1},{4,6},{5,7},{6,4},{7,5},{8,10},{9,11},{10,... | collective-permute-start | bytes 1572872 | tf_op jit(solution)/shard_map/ppermute | solution.py:305
  21.3 1.5 %collective-permute-start.4 = (bf16[2048,128]{1,0:T(8,128)(2,1)S(1)}, bf16[2048,128]{1,0:T(8,128)(2,1)S(1)}, u32[]{:S(2)}, u32[]{:S(2)}) collective-permute-start(bf16[2048,128]{1,0:T(8,128)(2,1)S(1)} %pad_maximum_fusion.refs_4_), channel_id=1, source_target_pairs={{0,8},{4,12},{8,0},{12,4},{1,9},{5,13},{9,1},{13,5},{2,10},{6,14},... | collective-permute-start | bytes 1572872 | tf_op jit(solution)/shard_map/ppermute | solution.py:309
  22.7 0.0 collective-permute-done.6.refs_5_
  22.7 0.0 collective-permute-done.7.refs_6_
  22.7 8.2 %attend_first.1 = (f32[4,1,640]{2,1,0:T(1,128)S(1)}, f32[4,1,640]{2,1,0:T(1,128)S(1)}, f32[4,128,640]{2,1,0:T(8,128)S(1)}) custom-call(s32[8,72]{1,0:T(8,128)S(1)} %tables.1.table_ref, bf16[128,2560]{1,0:T(8,128)(2,1)} %queries_ref.7, bf16[1664,128]{1,0:T(8,128)(2,1)S(1)} %collective-permute-done.1.refs_0_, ...), custom_call_target="tpu_custom_call" | custom-call | bytes 100000000 | tf_op jit(solution)/shard_map/attend_first/pallas_call | solution.py:231
  31.0 4.9 %collective-permute-done.5.refs_4_.refs_3_ = bf16[2048,128]{1,0:T(8,128)(2,1)S(1)} collective-permute-done((bf16[2048,128]{1,0:T(8,128)(2,1)S(1)}, bf16[2048,128]{1,0:T(8,128)(2,1)S(1)}, u32[]{:S(2)}, u32[]{:S(2)}) %collective-permute-start.5) | collective-permute-done | bytes 524320 | tf_op jit(solution)/shard_map/ppermute | solution.py:305
  35.9 0.0 collective-permute-done.4.refs_2_.refs_1_
  35.9 0.0 collective-permute-start.8
  35.9 0.5 collective-permute-start.9
  36.4 1.4 %collective-permute-done.8.refs_3_.refs_2_ = bf16[2048,128]{1,0:T(8,128)(2,1)S(1)} collective-permute-done((bf16[2048,128]{1,0:T(8,128)(2,1)S(1)}, bf16[2048,128]{1,0:T(8,128)(2,1)S(1)}, u32[]{:S(2)}, u32[]{:S(2)}) %collective-permute-start.8) | collective-permute-done | bytes 524320 | tf_op jit(solution)/shard_map/ppermute | solution.py:309
  37.8 0.7 %collective-permute-done.9.refs_5_.refs_4_ = bf16[2048,128]{1,0:T(8,128)(2,1)S(1)} collective-permute-done((bf16[2048,128]{1,0:T(8,128)(2,1)S(1)}, bf16[2048,128]{1,0:T(8,128)(2,1)S(1)}, u32[]{:S(2)}, u32[]{:S(2)}) %collective-permute-start.9) | collective-permute-done | bytes 524320 | tf_op jit(solution)/shard_map/ppermute | solution.py:309
  38.5 3.2 %attend_last.2 = (bf16[128,640]{1,0:T(8,128)(2,1)S(1)}, bf16[128,640]{1,0:T(8,128)(2,1)S(1)}) custom-call(s32[8,72]{1,0:T(8,128)S(1)} %tables.1.table_ref, bf16[128,2560]{1,0:T(8,128)(2,1)} %queries_ref.7, bf16[1664,128]{1,0:T(8,128)(2,1)S(1)} %collective-permute-done.1.refs_0_, bf16[1664,128]{1,0:T(8,128)(2,1)S(1)} %collective-permute-done.2.refs_2_.refs_1_, ...), custom_call_target="tpu_custom_call" | custom-call | bytes 100000000 | tf_op jit(solution)/shard_map/attend_last/pallas_call | solution.py:231
  41.7 3.6 %collective-permute-start.10 = (bf16[128,640]{1,0:T(8,128)(2,1)S(1)}, bf16[128,640]{1,0:T(8,128)(2,1)S(1)}, u32[]{:S(2)}, u32[]{:S(2)}) collective-permute-start(bf16[128,640]{1,0:T(8,128)(2,1)S(1)} %get-tuple-element.52), channel_id=1, source_target_pairs={{0,3},{1,0},{2,1},{3,2},{4,7},{5,4},{6,5},{7,6},{8,11},{9,8},{10,9... | collective-permute-start | bytes 491528 | tf_op jit(solution)/shard_map/ppermute | solution.py:305
  45.3 0.2 collective-permute-start.11
  45.5 4.6 %attend_last.3 = (bf16[128,640]{1,0:T(8,128)(2,1)S(1)}, bf16[128,2560]{1,0:T(8,128)(2,1)}) custom-call(s32[8,72]{1,0:T(8,128)S(1)} %tables.1.table_ref, bf16[128,2560]{1,0:T(8,128)(2,1)} %queries_ref.7, bf16[640,128]{1,0:T(8,128)(2,1)S(1)} %collective-permute-done.3.refs_1_.refs_0_, bf16[2048,128]{1,0:T(8,128)(2,1)S(1)} %collective-permute-done.4.refs_2_.refs_1_, ...), custom_call_target="tpu_custom_call" | custom-call | bytes 100000000 | tf_op jit(solution)/shard_map/attend_last/pallas_call | solution.py:231
  50.1 3.4 %collective-permute-done.11.refs_3_ = bf16[128,640]{1,0:T(8,128)(2,1)S(1)} collective-permute-done((bf16[128,640]{1,0:T(8,128)(2,1)S(1)}, bf16[128,640]{1,0:T(8,128)(2,1)S(1)}, u32[]{:S(2)}, u32[]{:S(2)}) %collective-permute-start.11) | collective-permute-done | bytes 163872 | tf_op jit(solution)/shard_map/ppermute | solution.py:305
  53.5 0.2 collective-permute-start.12
  53.7 7.4 %collective-permute-done.12.refs_2_ = bf16[128,640]{1,0:T(8,128)(2,1)S(1)} collective-permute-done((bf16[128,640]{1,0:T(8,128)(2,1)S(1)}, bf16[128,640]{1,0:T(8,128)(2,1)S(1)}, u32[]{:S(2)}, u32[]{:S(2)}) %collective-permute-start.12) | collective-permute-done | bytes 163872 | tf_op jit(solution)/shard_map/ppermute | solution.py:305
  61.0 0.8 %unpack.1 = bf16[128,2560]{1,0:T(8,128)(2,1)} custom-call(bf16[128,2560]{1,0:T(8,128)(2,1)} %get-tuple-element.57.refs_0_, bf16[128,640]{1,0:T(8,128)(2,1)S(1)} %collective-permute-done.10.refs_1_, bf16[128,640]{1,0:T(8,128)(2,1)S(1)} %collective-permute-done.12.refs_2_, ...), custom_call_target="tpu_custom_call", output_to_operand_aliasing={{}: (0, {})} | custom-call | tf_op jit(solution)/shard_map/unpack/pallas_call | solution.py:85
  (10 shorter events, 0.2 us)
Async XLA Ops:
  0.0 7.4 %copy-start = (s32[16,64]{1,0:T(8,128)S(1)}, s32[16,64]{1,0:T(8,128)}, u32[]{:S(2)}) copy-start(s32[16,64]{1,0:T(8,128)} %ancestry_ref.1) | copy-start | bytes 12292
  0.0 7.4 %copy-start.1 = (s32[16]{0:T(128)S(1)}, s32[16]{0:T(128)}, u32[]{:S(2)}) copy-start(s32[16]{0:T(128)} %leaf_tiles_ref.1) | copy-start | bytes 196
  1.6 17.9 %collective-permute-start = (bf16[2048,128]{1,0:T(8,128)(2,1)S(1)}, bf16[2048,128]{1,0:T(8,128)(2,1)S(1)}, u32[]{:S(2)}, u32[]{:S(2)}) collective-permute-start(bf16[2048,128]{1,0:T(8,128)(2,1)S(1)} %get-tuple-element.41), channel_id=1, source_target_pairs={{0,8},{4,12},{8,0},{12,4},{1,9},{5,13},{9,1},{13,5},{2,10},{6,14},... | collective-permute-start | bytes 1572872 | tf_op jit(solution)/shard_map/ppermute | solution.py:309
  3.9 15.5 %collective-permute-start.1 = (bf16[1664,128]{1,0:T(8,128)(2,1)S(1)}, bf16[1664,128]{1,0:T(8,128)(2,1)S(1)}, u32[]{:S(2)}, u32[]{:S(2)}) collective-permute-start(bf16[1664,128]{1,0:T(8,128)(2,1)S(1)} %get-tuple-element.35), channel_id=1, source_target_pairs={{0,1},{1,2},{2,3},{3,0},{4,5},{5,6},{6,7},{7,4},{8,9},{9,10},{10,1... | collective-permute-start | bytes 1277960 | tf_op jit(solution)/shard_map/ppermute | solution.py:305
  4.0 15.5 %collective-permute-start.2 = (bf16[1664,128]{1,0:T(8,128)(2,1)S(1)}, bf16[1664,128]{1,0:T(8,128)(2,1)S(1)}, u32[]{:S(2)}, u32[]{:S(2)}) collective-permute-start(bf16[1664,128]{1,0:T(8,128)(2,1)S(1)} %get-tuple-element.36), channel_id=1, source_target_pairs={{0,3},{1,0},{2,1},{3,2},{4,7},{5,4},{6,5},{7,6},{8,11},{9,8},{10,9... | collective-permute-start | bytes 1277960 | tf_op jit(solution)/shard_map/ppermute | solution.py:305
  7.2 12.3 %collective-permute-start.3 = (bf16[640,128]{1,0:T(8,128)(2,1)S(1)}, bf16[640,128]{1,0:T(8,128)(2,1)S(1)}, u32[]{:S(2)}, u32[]{:S(2)}) collective-permute-start(bf16[640,128]{1,0:T(8,128)(2,1)S(1)} %get-tuple-element.37), channel_id=1, source_target_pairs={{0,2},{1,3},{2,0},{3,1},{4,6},{5,7},{6,4},{7,5},{8,10},{9,11},{10,... | collective-permute-start | bytes 491528 | tf_op jit(solution)/shard_map/ppermute | solution.py:305
  19.6 3.1 %collective-permute-start.6 = (bf16[2048,128]{1,0:T(8,128)(2,1)S(1)}, bf16[2048,128]{1,0:T(8,128)(2,1)S(1)}, u32[]{:S(2)}, u32[]{:S(2)}) collective-permute-start(bf16[2048,128]{1,0:T(8,128)(2,1)S(1)} %pad_maximum_fusion.2.refs_3_), channel_id=1, source_target_pairs={{0,4},{4,0},{8,12},{12,8},{1,5},{5,1},{9,13},{13,9},{2,6},{6,2},{1... | collective-permute-start | bytes 1572872 | tf_op jit(solution)/shard_map/ppermute | solution.py:309
  19.8 2.9 %collective-permute-start.7 = (bf16[2048,128]{1,0:T(8,128)(2,1)S(1)}, bf16[2048,128]{1,0:T(8,128)(2,1)S(1)}, u32[]{:S(2)}, u32[]{:S(2)}) collective-permute-start(bf16[2048,128]{1,0:T(8,128)(2,1)S(1)} %pad_maximum_fusion.refs_4_), channel_id=1, source_target_pairs={{0,4},{4,0},{8,12},{12,8},{1,5},{5,1},{9,13},{13,9},{2,6},{6,2},{1... | collective-permute-start | bytes 1572872 | tf_op jit(solution)/shard_map/ppermute | solution.py:309
  20.4 15.4 %collective-permute-start.5 = (bf16[2048,128]{1,0:T(8,128)(2,1)S(1)}, bf16[2048,128]{1,0:T(8,128)(2,1)S(1)}, u32[]{:S(2)}, u32[]{:S(2)}) collective-permute-start(bf16[2048,128]{1,0:T(8,128)(2,1)S(1)} %pad_maximum_fusion.1), channel_id=1, source_target_pairs={{0,2},{1,3},{2,0},{3,1},{4,6},{5,7},{6,4},{7,5},{8,10},{9,11},{10,... | collective-permute-start | bytes 1572872 | tf_op jit(solution)/shard_map/ppermute | solution.py:305
  21.3 14.6 %collective-permute-start.4 = (bf16[2048,128]{1,0:T(8,128)(2,1)S(1)}, bf16[2048,128]{1,0:T(8,128)(2,1)S(1)}, u32[]{:S(2)}, u32[]{:S(2)}) collective-permute-start(bf16[2048,128]{1,0:T(8,128)(2,1)S(1)} %pad_maximum_fusion.refs_4_), channel_id=1, source_target_pairs={{0,8},{4,12},{8,0},{12,4},{1,9},{5,13},{9,1},{13,5},{2,10},{6,14},... | collective-permute-start | bytes 1572872 | tf_op jit(solution)/shard_map/ppermute | solution.py:309
  35.9 1.9 %collective-permute-start.8 = (bf16[2048,128]{1,0:T(8,128)(2,1)S(1)}, bf16[2048,128]{1,0:T(8,128)(2,1)S(1)}, u32[]{:S(2)}, u32[]{:S(2)}) collective-permute-start(bf16[2048,128]{1,0:T(8,128)(2,1)S(1)} %collective-permute-done.4.refs_2_.refs_1_), channel_id=1, source_target_pairs={{0,4},{4,0},{8,12},{12,8},{1,5},{5,1},{9,13},{13,9},{2,6},{6,2},{1... | collective-permute-start | bytes 1572872 | tf_op jit(solution)/shard_map/ppermute | solution.py:309
  35.9 2.7 %collective-permute-start.9 = (bf16[2048,128]{1,0:T(8,128)(2,1)S(1)}, bf16[2048,128]{1,0:T(8,128)(2,1)S(1)}, u32[]{:S(2)}, u32[]{:S(2)}) collective-permute-start(bf16[2048,128]{1,0:T(8,128)(2,1)S(1)} %collective-permute-done.5.refs_4_.refs_3_), channel_id=1, source_target_pairs={{0,4},{4,0},{8,12},{12,8},{1,5},{5,1},{9,13},{13,9},{2,6},{6,2},{1... | collective-permute-start | bytes 1572872 | tf_op jit(solution)/shard_map/ppermute | solution.py:309
  41.7 8.4 %collective-permute-start.10 = (bf16[128,640]{1,0:T(8,128)(2,1)S(1)}, bf16[128,640]{1,0:T(8,128)(2,1)S(1)}, u32[]{:S(2)}, u32[]{:S(2)}) collective-permute-start(bf16[128,640]{1,0:T(8,128)(2,1)S(1)} %get-tuple-element.52), channel_id=1, source_target_pairs={{0,3},{1,0},{2,1},{3,2},{4,7},{5,4},{6,5},{7,6},{8,11},{9,8},{10,9... | collective-permute-start | bytes 491528 | tf_op jit(solution)/shard_map/ppermute | solution.py:305
  45.3 8.1 %collective-permute-start.11 = (bf16[128,640]{1,0:T(8,128)(2,1)S(1)}, bf16[128,640]{1,0:T(8,128)(2,1)S(1)}, u32[]{:S(2)}, u32[]{:S(2)}) collective-permute-start(bf16[128,640]{1,0:T(8,128)(2,1)S(1)} %get-tuple-element.59), channel_id=1, source_target_pairs={{0,1},{1,2},{2,3},{3,0},{4,5},{5,6},{6,7},{7,4},{8,9},{9,10},{10,1... | collective-permute-start | bytes 491528 | tf_op jit(solution)/shard_map/ppermute | solution.py:305
  53.5 7.6 %collective-permute-start.12 = (bf16[128,640]{1,0:T(8,128)(2,1)S(1)}, bf16[128,640]{1,0:T(8,128)(2,1)S(1)}, u32[]{:S(2)}, u32[]{:S(2)}) collective-permute-start(bf16[128,640]{1,0:T(8,128)(2,1)S(1)} %get-tuple-element.61), channel_id=1, source_target_pairs={{0,2},{1,3},{2,0},{3,1},{4,6},{5,7},{6,4},{7,5},{8,10},{9,11},{10,... | collective-permute-start | bytes 491528 | tf_op jit(solution)/shard_map/ppermute | solution.py:305
where the time goes:
time: 61.7 us; the launch traced here: 62 us
  waiting for transfers between devices  24.2 us (39%)
  Pallas kernels  23.9 us (39%)
  starting transfers between devices  13.3 us (22%)
    ppermute x7, waiting for transfers between devices, turn(): lax.ppermute(array, 'kv', [(i, (i + by) % RING) for i in range(RING)])  22.1 us
    pallas_call x3, Pallas kernels, attend(): pl.pallas_call(functools.partial(attend_kernel, steps, last, len(kv_parts...  16 us
    ppermute x7, starting transfers between devices, turn(): lax.ppermute(array, 'kv', [(i, (i + by) % RING) for i in range(RING)])  8.26 us
    pallas_call x1, Pallas kernels, chain_tables(): pl.pallas_call(tables_kernel, out_shape=jax.ShapeDtypeStruct((2 * RING, a...  5.56 us
    ppermute x6, starting transfers between devices, across(): return lax.ppermute(array, 'blk', [(i, i ^ bit) for i in range(BLKS)])  5.03 us
    ppermute x6, waiting for transfers between devices, across(): return lax.ppermute(array, 'blk', [(i, i ^ bit) for i in range(BLKS)])  2.16 us
    pallas_call x1, Pallas kernels, pack(): pl.pallas_call(pack_kernel, out_shape=[pltpu.VMEM((length, DH), jnp.bfloa...  1.58 us
  transfers between devices with their start and end apart: 13, of which 6 were waited for; matrix products, arithmetic and copies ran while one was open for 0% of the time, Pallas kernels for 30%

commit v1 on v0

v1 whole, which is shorter than its diff:
```python
import functools
import math

import jax
import jax.numpy as jnp
from jax import lax
from jax.experimental import pallas as pl
from jax.experimental.pallas import tpu as pltpu
from jax.sharding import PartitionSpec as P

TILE = 128
KV_HEADS = 4
GROUP = 5
DH = 128
WIDE = GROUP * DH
RING = 4
BLKS = 4
GROUPS = 3
LOW = -1e30
SCALE = math.log2(math.e) / math.sqrt(DH)


def in_hbm(array):
    return pltpu.with_memory_space_constraint(array, pltpu.HBM)


def in_vmem(array):
    return pltpu.with_memory_space_constraint(array, pltpu.VMEM)


def pack_kernel(queries_ref, keys_ref, values_ref, across_ref, first_ref, third_ref, q_ref, sems):
    me = lax.axis_index("kv")
    rows = keys_ref.shape[0]
    copies = []

    def move(source, target):
        copies.append(pltpu.make_async_copy(source, target, sems.at[len(copies)]))
        copies[-1].start()

    for step, target, start in ((0, across_ref, 0), (2, across_ref, 2 * rows), (1, first_ref, 0), (3, third_ref, 0)):
        head = lax.rem(me + step, RING)
        narrow = pl.ds(pl.multiple_of(head * DH, DH), DH)
        move(keys_ref.at[:, narrow], target.at[pl.ds(start, rows)])
        move(values_ref.at[:, narrow], target.at[pl.ds(start + rows, rows)])
    for step, target, start in ((1, first_ref, 2 * rows), (3, third_ref, 2 * rows), (2, q_ref, 0)):
        head = lax.rem(me + step, RING)
        for g in range(GROUP):
            narrow = pl.ds(pl.multiple_of((head * GROUP + g) * DH, DH), DH)
            move(queries_ref.at[:, narrow], target.at[pl.ds(start + g * TILE, TILE)])
    for copy in copies:
        copy.wait()


def pack(queries, keys, values):
    rows = 2 * keys.shape[0]
    hbm = pl.BlockSpec(memory_space=pltpu.HBM)
    vmem = pl.BlockSpec(memory_space=pltpu.VMEM)
    lengths = (2 * rows, rows + WIDE, rows + WIDE, WIDE)
    return pl.pallas_call(
        pack_kernel,
        out_shape=[pltpu.VMEM((length, DH), jnp.bfloat16) for length in lengths],
        in_specs=[hbm] * 3,
        out_specs=[vmem] * len(lengths),
        scratch_shapes=[pltpu.SemaphoreType.DMA((2 * RING + 3 * GROUP,))],
        compiler_params=pltpu.CompilerParams(vmem_limit_bytes=4 * 1024 * 1024),
        name="pack",
    )(in_hbm(queries), in_hbm(keys), in_hbm(values))


def unpack_kernel(*refs):
    parts, out_ref, sems = refs[:RING], refs[RING], refs[RING + 1]
    me = lax.axis_index("kv")
    copies = []
    for step in range(RING):
        wide = pl.ds(pl.multiple_of(lax.rem(me + step, RING) * WIDE, DH), WIDE)
        copies.append(pltpu.make_async_copy(parts[step], out_ref.at[:, wide], sems.at[step]))
    for copy in copies:
        copy.start()
    for copy in copies:
        copy.wait()


def unpack(parts):
    return pl.pallas_call(
        unpack_kernel,
        out_shape=pltpu.HBM((TILE, KV_HEADS * WIDE), jnp.bfloat16),
        in_specs=[pl.BlockSpec(memory_space=pltpu.VMEM)] * RING,
        out_specs=pl.BlockSpec(memory_space=pltpu.HBM),
        scratch_shapes=[pltpu.SemaphoreType.DMA((RING,))],
        compiler_params=pltpu.CompilerParams(vmem_limit_bytes=4 * 1024 * 1024),
        name="unpack",
    )(*[in_vmem(part) for part in parts])


def attend_kernel(group, parts, table_ref, *refs):
    q_refs, refs = list(refs[:RING]), refs[RING:]
    kv_refs, refs = refs[:parts], refs[parts:]
    fetches = []
    if group == 0:
        peaks, totals, sums, own_queries, held, sems = refs
        me = lax.axis_index("kv")
        for g in range(GROUP):
            narrow = pl.ds(pl.multiple_of((me * GROUP + g) * DH, DH), DH)
            fetches.append(
                pltpu.make_async_copy(q_refs[0].at[:, narrow], own_queries.at[pl.ds(g * TILE, TILE)], sems.at[g])
            )
            fetches[-1].start()
        q_refs[0] = own_queries
    else:
        (peaks, totals, sums), o_refs, held = refs[3:6], refs[6:-1], refs[-1]
    place, rows = 0, held.shape[1]
    for kv_ref in kv_refs:
        for i in range(kv_ref.shape[0] // rows):
            held[place] = kv_ref[i * rows : (i + 1) * rows]
            place += 1
    rows = rows // 2
    tiles_each = rows // TILE
    ahead = lax.broadcasted_iota(jnp.int32, (TILE, TILE), 0) > lax.broadcasted_iota(jnp.int32, (TILE, TILE), 1)
    ahead = jnp.concatenate([ahead] * GROUP, axis=1)
    for fetch in fetches:
        fetch.wait()

    def tiles_of(which, slots):
        found = []
        for slot in slots:
            row = pl.multiple_of((slot % tiles_each) * TILE, TILE)
            found.append(held[slot // tiles_each, pl.ds(row + which * rows, TILE), :])
        return jnp.concatenate(found, axis=0)

    def visit(step, slots, shown, own, carried):
        peak, total, summed = carried
        q_ref = q_refs[step]
        raw = lax.dot_general(
            tiles_of(0, slots),
            q_ref[q_ref.shape[0] - WIDE :],
            (((1,), (1,)), ((), ())),
            preferred_element_type=jnp.float32,
        )
        if own:
            raw = jnp.where(ahead, LOW, raw)
        raw = [raw[i * TILE : (i + 1) * TILE] for i in range(len(slots))]
        higher = peak
        for part, show in zip(raw, shown):
            higher = jnp.maximum(higher, jnp.where(show, jnp.max(part, axis=0, keepdims=True), LOW))
        shift = higher * SCALE
        kept = jnp.exp2(peak * SCALE - shift)
        weights = [jnp.exp2(part * SCALE - jnp.where(show, shift, -LOW)) for part, show in zip(raw, shown)]
        total = total * kept
        for part in weights:
            total = total + jnp.sum(part, axis=0, keepdims=True)
        update = lax.dot_general(
            tiles_of(1, slots),
            jnp.concatenate(weights, axis=0).astype(jnp.bfloat16),
            (((0,), (0,)), ((), ())),
            preferred_element_type=jnp.float32,
        )
        return (higher, total, summed * kept + update)

    def add(step, slots, shown, own):
        carried = visit(step, slots, shown, own, (peaks[step], totals[step], sums[step]))
        for ref, value in zip((peaks, totals, sums), carried):
            ref[step] = value

    if group == 0:
        peaks[...] = jnp.full(peaks.shape, LOW, jnp.float32)
        totals[...] = jnp.zeros(totals.shape, jnp.float32)
        sums[...] = jnp.zeros(sums.shape, jnp.float32)
    for step in range(RING):
        row = step + RING * group
        if group == 0:
            add(step, [table_ref[row, 2]], [table_ref[row, 1] == 1], True)
        else:
            pl.when(table_ref[row, 1] == 1)(functools.partial(add, step, [table_ref[row, 2]], [True], True))

    fulls = [table_ref[step + RING * group, 0] for step in range(RING)]
    most = functools.reduce(jnp.maximum, fulls)

    def round_of(start, width, at, carry):
        for step in range(RING):
            tiles = [start + width * at + place for place in range(width)]
            slots = [table_ref[step + RING * group, 3 + tile] for tile in tiles]
            add(step, slots, [tile < fulls[step] for tile in tiles], False)
        return carry

    fours = (most + 1) // 4
    lax.fori_loop(0, fours, functools.partial(round_of, 0, 4), 0)
    lax.fori_loop(0, (most - 4 * fours + 1) // 2, functools.partial(round_of, 4 * fours, 2), 0)

    if group == GROUPS - 1:
        for step in range(RING):
            result = sums[step] / totals[step]
            for g in range(GROUP):
                o_refs[step][:, g * DH : (g + 1) * DH] = (
                    result[:, g * TILE : (g + 1) * TILE].T.astype(jnp.bfloat16)
                )


def attend(group, table, query_parts, kv_parts, state, cost):
    rows = 2 * TILE * 4
    blocks = sum(part.shape[0] // rows for part in kv_parts)
    vmem = pl.BlockSpec(memory_space=pltpu.VMEM)
    smem = pl.BlockSpec(memory_space=pltpu.SMEM)
    hbm = pl.BlockSpec(memory_space=pltpu.HBM)
    operands = [table, *query_parts, *kv_parts, *state]
    in_specs = [smem] + [vmem] * (len(operands) - 1)
    outs = [pltpu.VMEM((RING, length, WIDE), jnp.float32) for length in (1, 1, DH)]
    scratch = [pltpu.VMEM((blocks, rows, DH), jnp.bfloat16)]
    aliases = {}
    if group == 0:
        operands[1], in_specs[1] = in_hbm(query_parts[0]), hbm
        outs.append(pltpu.VMEM((WIDE, DH), jnp.bfloat16))
        scratch.append(pltpu.SemaphoreType.DMA((GROUP,)))
    else:
        aliases = {len(operands) - 3 + i: i for i in range(3)}
    if group == GROUPS - 1:
        outs += [pltpu.VMEM((TILE, WIDE), jnp.bfloat16)] * RING
    return pl.pallas_call(
        functools.partial(attend_kernel, group, len(kv_parts)),
        out_shape=outs,
        in_specs=in_specs,
        out_specs=[vmem] * len(outs),
        input_output_aliases=aliases,
        scratch_shapes=scratch,
        compiler_params=pltpu.CompilerParams(vmem_limit_bytes=12 * 1024 * 1024),
        cost_estimate=pl.CostEstimate(flops=0, bytes_accessed=cost, transcendentals=0),
        name="attend",
    )(*operands)


def tables_kernel(ancestry_ref, leaf_tiles_ref, table_ref):
    me, blk = lax.axis_index("kv"), lax.axis_index("blk")
    tiles = ancestry_ref.shape[1]
    each = tiles // (BLKS * RING)
    query_tiles = [blk * RING + lax.rem(me - step + RING, RING) for step in range(RING)]

    def place_of(tile):
        owner = tile // each
        relative = (owner // RING) ^ blk
        turned = (me - owner) & (RING - 1)
        low, high = relative & 1, relative // 2
        early = (turned == 0) | ((high == 0) & (turned != 2))
        middle = (low == 0) & (turned != 2)
        group = jnp.where(early, 0, jnp.where(middle, 1, 2))
        early_block = low * RING + jnp.where(turned == 0, high, 2 + turned // 2)
        late_block = jnp.where(turned == 2, 2 + low * 2 + high, turned // 2)
        block = jnp.where(early, early_block, late_block)
        return group * RING, block * each + (tile & (each - 1))

    def visit(tile, carried):
        row, place = place_of(tile)
        for step in range(RING):
            count = table_ref[row + step, 0]
            table_ref[row + step, 3 + count] = place
            table_ref[row + step, 0] = count + ancestry_ref[query_tiles[step], tile]
        return carried

    def clear(at, carried):
        for row in range(GROUPS * RING):
            table_ref[row, at] = 0
        return carried

    lax.fori_loop(0, table_ref.shape[1], clear, 0)
    lax.fori_loop(0, tiles, visit, 0)
    for step in range(RING):
        row, place = place_of(leaf_tiles_ref[query_tiles[step]])
        table_ref[row + step, 1] = 1
        table_ref[row + step, 2] = place


def chain_tables(ancestry, leaf_tiles):
    smem = pl.BlockSpec(memory_space=pltpu.SMEM)
    return pl.pallas_call(
        tables_kernel,
        out_shape=jax.ShapeDtypeStruct((GROUPS * RING, ancestry.shape[1] // 2 + 8), jnp.int32),
        in_specs=[smem, smem],
        out_specs=smem,
        compiler_params=pltpu.CompilerParams(vmem_limit_bytes=1024 * 1024),
        cost_estimate=pl.CostEstimate(flops=0, bytes_accessed=10**8, transcendentals=0),
        name="tables",
    )(ancestry, leaf_tiles)


def turn(array, by):
    return lax.ppermute(array, "kv", [(i, (i + by) % RING) for i in range(RING)])


def across(array, bit):
    return lax.ppermute(array, "blk", [(i, i ^ bit) for i in range(BLKS)])


def on_device(queries, keys, values, ancestry, leaf_tiles):
    table = chain_tables(ancestry, leaf_tiles)
    sent_across, sent_first, sent_third, sent_queries = pack(queries, keys, values)
    block = 2 * keys.shape[0]

    got_first, got_third = turn(sent_first, 1), turn(sent_third, 3)
    got_across = across(sent_across, 2)
    got_queries = turn(sent_queries, 2)
    sent_across, got_across, got_first, got_third, got_queries, table = lax.optimization_barrier(
        (sent_across, got_across, got_first, got_third, got_queries, table)
    )
    query_parts = [queries, got_first, got_queries, got_third]

    got_last = turn(jnp.concatenate([sent_across[block:], got_across[block:]], axis=0), 2)
    own_sides = jnp.concatenate([got_first[:block], got_third[:block]], axis=0)
    far_sides = across(own_sides, 2)
    here = jnp.concatenate([sent_across[:block], got_across[:block]], axis=0)
    swapped_here, near_sides = across(here, 1), across(own_sides, 1)
    parts = [here, own_sides, swapped_here, near_sides]
    *state, query_parts[0] = attend(0, table, query_parts, parts, [], 10**8)

    far_sides, *state = lax.optimization_barrier((far_sides, *state))
    diagonal_sides = across(far_sides, 1)
    state = attend(1, table, query_parts, [far_sides], state, 10)
    got_last, *state = lax.optimization_barrier((got_last, *state))
    outs = attend(2, table, query_parts, [diagonal_sides, got_last, across(got_last, 1)], state, 10)[3:]
    return unpack([outs[0]] + [turn(outs[step], -step) for step in range(1, RING)])


def solution(mesh):
    in_specs = (
        P(("leaf", "blk", "kv"), None),
        P(("leaf", "blk", "kv"), None),
        P(("leaf", "blk", "kv"), None),
        P("leaf", None),
        P("leaf"),
    )
    out_specs = P(("leaf", "blk", "kv"), None)
    return jax.shard_map(
        on_device, mesh=mesh, in_specs=in_specs, out_specs=out_specs, check_vma=False
    )
```

time: 61.7 us -> 59.5 us (0.964); the launches traced: 62 us -> 58.6 us
  Pallas kernels: 23.9 us -> 21.5 us
  waiting for transfers between devices: 24.2 us -> 22.8 us
    ppermute x7, waiting for transfers between devices: 22.1 us -> 17.1 us  [turn(): lax.ppermute(array, 'kv', [(i, (i + by) % RING) for i in range(RING)])]
    ppermute x6, waiting for transfers between devices: 2.16 us -> 5.66 us  [across(): return lax.ppermute(array, 'blk', [(i, i ^ bit) for i in range(BLKS)])]
    pallas_call x4, Pallas kernels: 21.6 us -> 19 us  [the longest x3 13.5 us: attend(): pl.pallas_call(functools.partial(attend_kernel, group, len(kv_parts)), ou...]
    ppermute x7, starting transfers between devices: 8.26 us -> 9.35 us  [turn(): lax.ppermute(array, 'kv', [(i, (i + by) % RING) for i in range(RING)])]
  transfers between devices with their start and end apart: 13 -> 13, of which waited for: 6 -> 8; matrix products, arithmetic and copies ran while one was open for 0% -> 0% of each run, Pallas kernels for 30% -> 24%
where the time goes in v1:
time: 59.5 us; the launch traced here: 58.6 us
  waiting for transfers between devices  22.8 us (38%)
  Pallas kernels  21.5 us (36%)
  starting transfers between devices  13.9 us (23%)
    ppermute x7, waiting for transfers between devices, turn(): lax.ppermute(array, 'kv', [(i, (i + by) % RING) for i in range(RING)])  17.1 us
    pallas_call x3, Pallas kernels, attend(): pl.pallas_call(functools.partial(attend_kernel, group, len(kv_parts)), ou...  13.5 us
    ppermute x7, starting transfers between devices, turn(): lax.ppermute(array, 'kv', [(i, (i + by) % RING) for i in range(RING)])  9.35 us
    ppermute x6, waiting for transfers between devices, across(): return lax.ppermute(array, 'blk', [(i, i ^ bit) for i in range(BLKS)])  5.66 us
    pallas_call x1, Pallas kernels, chain_tables(): pl.pallas_call(tables_kernel, out_shape=jax.ShapeDtypeStruct((GROUPS * RI...  5.53 us
    ppermute x6, starting transfers between devices, across(): return lax.ppermute(array, 'blk', [(i, i ^ bit) for i in range(BLKS)])  4.54 us
    pallas_call x1, Pallas kernels, pack(): pl.pallas_call(pack_kernel, out_shape=[pltpu.VMEM((length, DH), jnp.bfloa...  1.58 us
  transfers between devices with their start and end apart: 13, of which 8 were waited for; matrix products, arithmetic and copies ran while one was open for 0% of the time, Pallas kernels for 24%

profile of v1, /device:TPU:2, one launch (start us, length us, event | category | flops | bytes accessed | tf_op | source)
XLA Modules:
  0.0 58.6 jit_solution(7126998209302470571)
XLA Ops:
  0.0 1.6 %pack.1 = (bf16[2048,128]{1,0:T(8,128)(2,1)S(1)}, bf16[1664,128]{1,0:T(8,128)(2,1)S(1)}, bf16[1664,128]{1,0:T(8,128)(2,1)S(1)}, bf16[640,128]{1,0:T(8,128)(2,1)S(1)}) custom-call(bf16[128,2560]{1,0:T(8,128)(2,1)} %refs_0_.1, bf16[512,512]{1,0:T(8,128)(2,1)} %keys_ref.1, bf16[512,512]{1,0:T(8,128)(2,1)} %values_ref.1), custom_call_target="tpu_custom_call" | custom-call | tf_op jit(solution)/shard_map/pack/pallas_call | solution.py:59
  1.6 2.4 %collective-permute-start = (bf16[2048,128]{1,0:T(8,128)(2,1)S(1)}, bf16[2048,128]{1,0:T(8,128)(2,1)S(1)}, u32[]{:S(2)}, u32[]{:S(2)}) collective-permute-start(bf16[2048,128]{1,0:T(8,128)(2,1)S(1)} %get-tuple-element.42), channel_id=1, source_target_pairs={{0,8},{4,12},{8,0},{12,4},{1,9},{5,13},{9,1},{13,5},{2,10},{6,14},... | collective-permute-start | bytes 1572872 | tf_op jit(solution)/shard_map/ppermute | solution.py:288
  3.9 0.0 collective-permute-start.1
  4.0 3.2 %collective-permute-start.2 = (bf16[1664,128]{1,0:T(8,128)(2,1)S(1)}, bf16[1664,128]{1,0:T(8,128)(2,1)S(1)}, u32[]{:S(2)}, u32[]{:S(2)}) collective-permute-start(bf16[1664,128]{1,0:T(8,128)(2,1)S(1)} %get-tuple-element.36), channel_id=1, source_target_pairs={{0,3},{1,0},{2,1},{3,2},{4,7},{5,4},{6,5},{7,6},{8,11},{9,8},{10,9... | collective-permute-start | bytes 1277960 | tf_op jit(solution)/shard_map/ppermute | solution.py:284
  7.2 0.2 collective-permute-start.3
  7.4 5.5 %tables.1.table_ref = s32[12,40]{1,0:T(8,128)S(1)} custom-call(s32[16,64]{1,0:T(8,128)S(1)} %copy-done, s32[16]{0:T(128)S(1)} %copy-done.1), custom_call_target="tpu_custom_call" | custom-call | bytes 100000000 | tf_op jit(solution)/shard_map/tables/pallas_call | solution.py:272
  13.0 6.5 %collective-permute-done.3.refs_2_ = bf16[640,128]{1,0:T(8,128)(2,1)S(1)} collective-permute-done((bf16[640,128]{1,0:T(8,128)(2,1)S(1)}, bf16[640,128]{1,0:T(8,128)(2,1)S(1)}, u32[]{:S(2)}, u32[]{:S(2)}) %collective-permute-start.3) | collective-permute-done | bytes 163872 | tf_op jit(solution)/shard_map/ppermute | solution.py:284
  19.5 0.0 collective-permute-done.1.refs_1_
  19.5 0.0 collective-permute-done.2.refs_3_
  19.6 1.6 %collective-permute-start.6 = (bf16[2048,128]{1,0:T(8,128)(2,1)S(1)}, bf16[2048,128]{1,0:T(8,128)(2,1)S(1)}, u32[]{:S(2)}, u32[]{:S(2)}) collective-permute-start(bf16[2048,128]{1,0:T(8,128)(2,1)S(1)} %pad_maximum_fusion.1.refs_5_), channel_id=1, source_target_pairs={{0,8},{4,12},{8,0},{12,4},{1,9},{5,13},{9,1},{13,5},{2,10},{6,14},... | collective-permute-start | bytes 1572872 | tf_op jit(solution)/shard_map/ppermute | solution.py:288
  21.1 0.0 collective-permute-start.5
  21.1 0.1 fusion
  21.3 0.6 %collective-permute-start.4 = (bf16[2048,128]{1,0:T(8,128)(2,1)S(1)}, bf16[2048,128]{1,0:T(8,128)(2,1)S(1)}, u32[]{:S(2)}, u32[]{:S(2)}) collective-permute-start(bf16[2048,128]{1,0:T(8,128)(2,1)S(1)} %pad_maximum_fusion.refs_4_), channel_id=1, source_target_pairs={{0,4},{4,0},{8,12},{12,8},{1,5},{5,1},{9,13},{13,9},{2,6},{6,2},{1... | collective-permute-start | bytes 1572872 | tf_op jit(solution)/shard_map/ppermute | solution.py:288
  21.9 0.8 %collective-permute-start.8 = (bf16[2048,128]{1,0:T(8,128)(2,1)S(1)}, bf16[2048,128]{1,0:T(8,128)(2,1)S(1)}, u32[]{:S(2)}, u32[]{:S(2)}) collective-permute-start(bf16[2048,128]{1,0:T(8,128)(2,1)S(1)} %pad_maximum_fusion.2), channel_id=1, source_target_pairs={{0,2},{1,3},{2,0},{3,1},{4,6},{5,7},{6,4},{7,5},{8,10},{9,11},{10,... | collective-permute-start | bytes 1572872 | tf_op jit(solution)/shard_map/ppermute | solution.py:284
  22.7 1.1 %collective-permute-done.4.refs_6_ = bf16[2048,128]{1,0:T(8,128)(2,1)S(1)} collective-permute-done((bf16[2048,128]{1,0:T(8,128)(2,1)S(1)}, bf16[2048,128]{1,0:T(8,128)(2,1)S(1)}, u32[]{:S(2)}, u32[]{:S(2)}) %collective-permute-start.4) | collective-permute-done | bytes 524320 | tf_op jit(solution)/shard_map/ppermute | solution.py:288
  23.8 0.0 collective-permute-done.5.refs_7_
  23.8 5.6 %attend.3 = (f32[4,1,640]{2,1,0:T(1,128)S(1)}, f32[4,1,640]{2,1,0:T(1,128)S(1)}, f32[4,128,640]{2,1,0:T(8,128)S(1)}, bf16[640,128]{1,0:T(8,128)(2,1)S(1)}) custom-call(s32[12,40]{1,0:T(8,128)S(1)} %tables.1.table_ref, bf16[128,2560]{1,0:T(8,128)(2,1)} %refs_0_.1, bf16[1664,128]{1,0:T(8,128)(2,1)S(1)} %collective-permute-done.1.refs_1_, ...), custom_call_target="tpu_custom_call" | custom-call | bytes 100000000 | tf_op jit(solution)/shard_map/attend/pallas_call | solution.py:217
  29.5 2.7 %collective-permute-done.6.refs_4_ = bf16[2048,128]{1,0:T(8,128)(2,1)S(1)} collective-permute-done((bf16[2048,128]{1,0:T(8,128)(2,1)S(1)}, bf16[2048,128]{1,0:T(8,128)(2,1)S(1)}, u32[]{:S(2)}, u32[]{:S(2)}) %collective-permute-start.6) | collective-permute-done | bytes 524320 | tf_op jit(solution)/shard_map/ppermute | solution.py:288
  32.1 0.0 collective-permute-start.7
  32.1 2.7 %attend.4 = (f32[4,1,640]{2,1,0:T(1,128)S(1)}, f32[4,1,640]{2,1,0:T(1,128)S(1)}, f32[4,128,640]{2,1,0:T(8,128)S(1)}) custom-call(s32[12,40]{1,0:T(8,128)S(1)} %tables.1.table_ref, bf16[640,128]{1,0:T(8,128)(2,1)S(1)} %get-tuple-element.44.refs_0_, ...), custom_call_target="tpu_custom_call", output_to_operand_aliasing={{0}: (6, {}), {1}: (7, {}), {2}: (8, {})} | custom-call | bytes 10 | tf_op jit(solution)/shard_map/attend/pallas_call | solution.py:217
  34.8 2.5 %collective-permute-done.8.refs_5_ = bf16[2048,128]{1,0:T(8,128)(2,1)S(1)} collective-permute-done((bf16[2048,128]{1,0:T(8,128)(2,1)S(1)}, bf16[2048,128]{1,0:T(8,128)(2,1)S(1)}, u32[]{:S(2)}, u32[]{:S(2)}) %collective-permute-start.8) | collective-permute-done | bytes 524320 | tf_op jit(solution)/shard_map/ppermute | solution.py:284
  37.3 0.0 collective-permute-start.9
  37.3 0.0 collective-permute-done.7.refs_4_
  37.3 1.9 %collective-permute-done.9.refs_6_ = bf16[2048,128]{1,0:T(8,128)(2,1)S(1)} collective-permute-done((bf16[2048,128]{1,0:T(8,128)(2,1)S(1)}, bf16[2048,128]{1,0:T(8,128)(2,1)S(1)}, u32[]{:S(2)}, u32[]{:S(2)}) %collective-permute-start.9) | collective-permute-done | bytes 524320 | tf_op jit(solution)/shard_map/ppermute | solution.py:288
  39.2 5.2 %attend.5 = (f32[4,1,640]{2,1,0:T(1,128)S(1)}, f32[4,1,640]{2,1,0:T(1,128)S(1)}, f32[4,128,640]{2,1,0:T(8,128)S(1)}, bf16[128,640]{1,0:T(8,128)(2,1)S(1)}, bf16[...) custom-call(s32[12,40]{1,0:T(8,128)S(1)} %tables.1.table_ref, ...), custom_call_target="tpu_custom_call", output_to_operand_aliasing={{0}: (8, {}), {1}: (9, {}), {2}: (10, {})} | custom-call | bytes 10 | tf_op jit(solution)/shard_map/attend/pallas_call | solution.py:217
  44.4 0.9 %collective-permute-start.10 = (bf16[128,640]{1,0:T(8,128)(2,1)S(1)}, bf16[128,640]{1,0:T(8,128)(2,1)S(1)}, u32[]{:S(2)}, u32[]{:S(2)}) collective-permute-start(bf16[128,640]{1,0:T(8,128)(2,1)S(1)} %get-tuple-element.60), channel_id=1, source_target_pairs={{0,3},{1,0},{2,1},{3,2},{4,7},{5,4},{6,5},{7,6},{8,11},{9,8},{10,9... | collective-permute-start | bytes 491528 | tf_op jit(solution)/shard_map/ppermute | solution.py:284
  45.3 4.1 %collective-permute-start.11 = (bf16[128,640]{1,0:T(8,128)(2,1)S(1)}, bf16[128,640]{1,0:T(8,128)(2,1)S(1)}, u32[]{:S(2)}, u32[]{:S(2)}) collective-permute-start(bf16[128,640]{1,0:T(8,128)(2,1)S(1)} %get-tuple-element.61), channel_id=1, source_target_pairs={{0,2},{1,3},{2,0},{3,1},{4,6},{5,7},{6,4},{7,5},{8,10},{9,11},{10,... | collective-permute-start | bytes 491528 | tf_op jit(solution)/shard_map/ppermute | solution.py:284
  49.5 0.0 collective-permute-start.12
  49.5 3.4 %collective-permute-done.10.refs_1_ = bf16[128,640]{1,0:T(8,128)(2,1)S(1)} collective-permute-done((bf16[128,640]{1,0:T(8,128)(2,1)S(1)}, bf16[128,640]{1,0:T(8,128)(2,1)S(1)}, u32[]{:S(2)}, u32[]{:S(2)}) %collective-permute-start.10) | collective-permute-done | bytes 163872 | tf_op jit(solution)/shard_map/ppermute | solution.py:284
  52.9 1.6 %collective-permute-done.11.refs_2_ = bf16[128,640]{1,0:T(8,128)(2,1)S(1)} collective-permute-done((bf16[128,640]{1,0:T(8,128)(2,1)S(1)}, bf16[128,640]{1,0:T(8,128)(2,1)S(1)}, u32[]{:S(2)}, u32[]{:S(2)}) %collective-permute-start.11) | collective-permute-done | bytes 163872 | tf_op jit(solution)/shard_map/ppermute | solution.py:284
  54.5 3.2 %collective-permute-done.12.refs_3_ = bf16[128,640]{1,0:T(8,128)(2,1)S(1)} collective-permute-done((bf16[128,640]{1,0:T(8,128)(2,1)S(1)}, bf16[128,640]{1,0:T(8,128)(2,1)S(1)}, u32[]{:S(2)}, u32[]{:S(2)}) %collective-permute-start.12) | collective-permute-done | bytes 163872 | tf_op jit(solution)/shard_map/ppermute | solution.py:284
  57.6 0.9 %unpack.1 = bf16[128,2560]{1,0:T(8,128)(2,1)} custom-call(bf16[128,640]{1,0:T(8,128)(2,1)S(1)} %get-tuple-element.59.refs_0_, bf16[128,640]{1,0:T(8,128)(2,1)S(1)} %collective-permute-done.10.refs_1_, bf16[128,640]{1,0:T(8,128)(2,1)S(1)} %collective-permute-done.11.refs_2_, bf16[128,640]{1,0:T(8,128)(2,1)S(1)} %collective-permute-done.12.refs_3_), custom_call_target="tpu_custom_call" | custom-call | tf_op jit(solution)/shard_map/unpack/pallas_call | solution.py:84
  (10 shorter events, 0.2 us)
Async XLA Ops:
  0.0 7.4 %copy-start.1 = (s32[16]{0:T(128)S(1)}, s32[16]{0:T(128)}, u32[]{:S(2)}) copy-start(s32[16]{0:T(128)} %leaf_tiles_ref.1) | copy-start | bytes 196
  0.0 7.4 %copy-start = (s32[16,64]{1,0:T(8,128)S(1)}, s32[16,64]{1,0:T(8,128)}, u32[]{:S(2)}) copy-start(s32[16,64]{1,0:T(8,128)} %ancestry_ref.1) | copy-start | bytes 12292
  1.6 17.9 %collective-permute-start = (bf16[2048,128]{1,0:T(8,128)(2,1)S(1)}, bf16[2048,128]{1,0:T(8,128)(2,1)S(1)}, u32[]{:S(2)}, u32[]{:S(2)}) collective-permute-start(bf16[2048,128]{1,0:T(8,128)(2,1)S(1)} %get-tuple-element.42), channel_id=1, source_target_pairs={{0,8},{4,12},{8,0},{12,4},{1,9},{5,13},{9,1},{13,5},{2,10},{6,14},... | collective-permute-start | bytes 1572872 | tf_op jit(solution)/shard_map/ppermute | solution.py:288
  3.9 15.5 %collective-permute-start.1 = (bf16[1664,128]{1,0:T(8,128)(2,1)S(1)}, bf16[1664,128]{1,0:T(8,128)(2,1)S(1)}, u32[]{:S(2)}, u32[]{:S(2)}) collective-permute-start(bf16[1664,128]{1,0:T(8,128)(2,1)S(1)} %get-tuple-element.35), channel_id=1, source_target_pairs={{0,1},{1,2},{2,3},{3,0},{4,5},{5,6},{6,7},{7,4},{8,9},{9,10},{10,1... | collective-permute-start | bytes 1277960 | tf_op jit(solution)/shard_map/ppermute | solution.py:284
  4.0 15.5 %collective-permute-start.2 = (bf16[1664,128]{1,0:T(8,128)(2,1)S(1)}, bf16[1664,128]{1,0:T(8,128)(2,1)S(1)}, u32[]{:S(2)}, u32[]{:S(2)}) collective-permute-start(bf16[1664,128]{1,0:T(8,128)(2,1)S(1)} %get-tuple-element.36), channel_id=1, source_target_pairs={{0,3},{1,0},{2,1},{3,2},{4,7},{5,4},{6,5},{7,6},{8,11},{9,8},{10,9... | collective-permute-start | bytes 1277960 | tf_op jit(solution)/shard_map/ppermute | solution.py:284
  7.2 12.3 %collective-permute-start.3 = (bf16[640,128]{1,0:T(8,128)(2,1)S(1)}, bf16[640,128]{1,0:T(8,128)(2,1)S(1)}, u32[]{:S(2)}, u32[]{:S(2)}) collective-permute-start(bf16[640,128]{1,0:T(8,128)(2,1)S(1)} %get-tuple-element.37), channel_id=1, source_target_pairs={{0,2},{1,3},{2,0},{3,1},{4,6},{5,7},{6,4},{7,5},{8,10},{9,11},{10,... | collective-permute-start | bytes 491528 | tf_op jit(solution)/shard_map/ppermute | solution.py:284
  19.6 12.6 %collective-permute-start.6 = (bf16[2048,128]{1,0:T(8,128)(2,1)S(1)}, bf16[2048,128]{1,0:T(8,128)(2,1)S(1)}, u32[]{:S(2)}, u32[]{:S(2)}) collective-permute-start(bf16[2048,128]{1,0:T(8,128)(2,1)S(1)} %pad_maximum_fusion.1.refs_5_), channel_id=1, source_target_pairs={{0,8},{4,12},{8,0},{12,4},{1,9},{5,13},{9,1},{13,5},{2,10},{6,14},... | collective-permute-start | bytes 1572872 | tf_op jit(solution)/shard_map/ppermute | solution.py:288
  21.1 2.7 %collective-permute-start.5 = (bf16[2048,128]{1,0:T(8,128)(2,1)S(1)}, bf16[2048,128]{1,0:T(8,128)(2,1)S(1)}, u32[]{:S(2)}, u32[]{:S(2)}) collective-permute-start(bf16[2048,128]{1,0:T(8,128)(2,1)S(1)} %pad_maximum_fusion.1.refs_5_), channel_id=1, source_target_pairs={{0,4},{4,0},{8,12},{12,8},{1,5},{5,1},{9,13},{13,9},{2,6},{6,2},{1... | collective-permute-start | bytes 1572872 | tf_op jit(solution)/shard_map/ppermute | solution.py:288
  21.3 2.5 %collective-permute-start.4 = (bf16[2048,128]{1,0:T(8,128)(2,1)S(1)}, bf16[2048,128]{1,0:T(8,128)(2,1)S(1)}, u32[]{:S(2)}, u32[]{:S(2)}) collective-permute-start(bf16[2048,128]{1,0:T(8,128)(2,1)S(1)} %pad_maximum_fusion.refs_4_), channel_id=1, source_target_pairs={{0,4},{4,0},{8,12},{12,8},{1,5},{5,1},{9,13},{13,9},{2,6},{6,2},{1... | collective-permute-start | bytes 1572872 | tf_op jit(solution)/shard_map/ppermute | solution.py:288
  21.9 15.4 %collective-permute-start.8 = (bf16[2048,128]{1,0:T(8,128)(2,1)S(1)}, bf16[2048,128]{1,0:T(8,128)(2,1)S(1)}, u32[]{:S(2)}, u32[]{:S(2)}) collective-permute-start(bf16[2048,128]{1,0:T(8,128)(2,1)S(1)} %pad_maximum_fusion.2), channel_id=1, source_target_pairs={{0,2},{1,3},{2,0},{3,1},{4,6},{5,7},{6,4},{7,5},{8,10},{9,11},{10,... | collective-permute-start | bytes 1572872 | tf_op jit(solution)/shard_map/ppermute | solution.py:284
  32.1 5.2 %collective-permute-start.7 = (bf16[2048,128]{1,0:T(8,128)(2,1)S(1)}, bf16[2048,128]{1,0:T(8,128)(2,1)S(1)}, u32[]{:S(2)}, u32[]{:S(2)}) collective-permute-start(bf16[2048,128]{1,0:T(8,128)(2,1)S(1)} %collective-permute-done.6.refs_4_), channel_id=1, source_target_pairs={{0,4},{4,0},{8,12},{12,8},{1,5},{5,1},{9,13},{13,9},{2,6},{6,2},{1... | collective-permute-start | bytes 1572872 | tf_op jit(solution)/shard_map/ppermute | solution.py:288
  37.3 1.9 %collective-permute-start.9 = (bf16[2048,128]{1,0:T(8,128)(2,1)S(1)}, bf16[2048,128]{1,0:T(8,128)(2,1)S(1)}, u32[]{:S(2)}, u32[]{:S(2)}) collective-permute-start(bf16[2048,128]{1,0:T(8,128)(2,1)S(1)} %collective-permute-done.8.refs_5_), channel_id=1, source_target_pairs={{0,4},{4,0},{8,12},{12,8},{1,5},{5,1},{9,13},{13,9},{2,6},{6,2},{1... | collective-permute-start | bytes 1572872 | tf_op jit(solution)/shard_map/ppermute | solution.py:288
  44.4 8.5 %collective-permute-start.10 = (bf16[128,640]{1,0:T(8,128)(2,1)S(1)}, bf16[128,640]{1,0:T(8,128)(2,1)S(1)}, u32[]{:S(2)}, u32[]{:S(2)}) collective-permute-start(bf16[128,640]{1,0:T(8,128)(2,1)S(1)} %get-tuple-element.60), channel_id=1, source_target_pairs={{0,3},{1,0},{2,1},{3,2},{4,7},{5,4},{6,5},{7,6},{8,11},{9,8},{10,9... | collective-permute-start | bytes 491528 | tf_op jit(solution)/shard_map/ppermute | solution.py:284
  45.3 9.1 %collective-permute-start.11 = (bf16[128,640]{1,0:T(8,128)(2,1)S(1)}, bf16[128,640]{1,0:T(8,128)(2,1)S(1)}, u32[]{:S(2)}, u32[]{:S(2)}) collective-permute-start(bf16[128,640]{1,0:T(8,128)(2,1)S(1)} %get-tuple-element.61), channel_id=1, source_target_pairs={{0,2},{1,3},{2,0},{3,1},{4,6},{5,7},{6,4},{7,5},{8,10},{9,11},{10,... | collective-permute-start | bytes 491528 | tf_op jit(solution)/shard_map/ppermute | solution.py:284
  49.5 8.2 %collective-permute-start.12 = (bf16[128,640]{1,0:T(8,128)(2,1)S(1)}, bf16[128,640]{1,0:T(8,128)(2,1)S(1)}, u32[]{:S(2)}, u32[]{:S(2)}) collective-permute-start(bf16[128,640]{1,0:T(8,128)(2,1)S(1)} %get-tuple-element.62), channel_id=1, source_target_pairs={{0,1},{1,2},{2,3},{3,0},{4,5},{5,6},{6,7},{7,4},{8,9},{9,10},{10,1... | collective-permute-start | bytes 491528 | tf_op jit(solution)/shard_map/ppermute | solution.py:284

commit v2 on v1

--- a/solution.py
+++ b/solution.py
@@ -28,7 +28,7 @@
     return pltpu.with_memory_space_constraint(array, pltpu.VMEM)
 
 
-def pack_kernel(queries_ref, keys_ref, values_ref, across_ref, first_ref, third_ref, q_ref, sems):
+def pack_kernel(queries_ref, keys_ref, values_ref, here_ref, opposite_ref, first_ref, third_ref, q_ref, sems):
     me = lax.axis_index("kv")
     rows = keys_ref.shape[0]
     copies = []
@@ -37,11 +37,11 @@
         copies.append(pltpu.make_async_copy(source, target, sems.at[len(copies)]))
         copies[-1].start()
 
-    for step, target, start in ((0, across_ref, 0), (2, across_ref, 2 * rows), (1, first_ref, 0), (3, third_ref, 0)):
+    for step, target in ((1, first_ref), (3, third_ref), (0, here_ref), (2, opposite_ref)):
         head = lax.rem(me + step, RING)
         narrow = pl.ds(pl.multiple_of(head * DH, DH), DH)
-        move(keys_ref.at[:, narrow], target.at[pl.ds(start, rows)])
-        move(values_ref.at[:, narrow], target.at[pl.ds(start + rows, rows)])
+        move(keys_ref.at[:, narrow], target.at[pl.ds(0, rows)])
+        move(values_ref.at[:, narrow], target.at[pl.ds(rows, rows)])
     for step, target, start in ((1, first_ref, 2 * rows), (3, third_ref, 2 * rows), (2, q_ref, 0)):
         head = lax.rem(me + step, RING)
         for g in range(GROUP):
@@ -55,7 +55,7 @@
     rows = 2 * keys.shape[0]
     hbm = pl.BlockSpec(memory_space=pltpu.HBM)
     vmem = pl.BlockSpec(memory_space=pltpu.VMEM)
-    lengths = (2 * rows, rows + WIDE, rows + WIDE, WIDE)
+    lengths = (rows, rows, rows + WIDE, rows + WIDE, WIDE)
     return pl.pallas_call(
         pack_kernel,
         out_shape=[pltpu.VMEM((length, DH), jnp.bfloat16) for length in lengths],
@@ -172,23 +172,22 @@
         else:
             pl.when(table_ref[row, 1] == 1)(functools.partial(add, step, [table_ref[row, 2]], [True], True))
 
-    fulls = [table_ref[step + RING * group, 0] for step in range(RING)]
-    most = functools.reduce(jnp.maximum, fulls)
-
-    def round_of(start, width, at, carry):
-        for step in range(RING):
+    def round_of(steps, start, width, at, carry):
+        for step in steps:
             tiles = [start + width * at + place for place in range(width)]
             slots = [table_ref[step + RING * group, 3 + tile] for tile in tiles]
-            add(step, slots, [tile < fulls[step] for tile in tiles], False)
+            add(step, slots, [tile < table_ref[step + RING * group, 0] for tile in tiles], False)
         return carry
 
-    fours = (most + 1) // 4
-    lax.fori_loop(0, fours, functools.partial(round_of, 0, 4), 0)
-    lax.fori_loop(0, (most - 4 * fours + 1) // 2, functools.partial(round_of, 4 * fours, 2), 0)
+    for steps in ((0, 1), (2, 3)):
+        most = functools.reduce(jnp.maximum, [table_ref[step + RING * group, 0] for step in steps])
+        fours = (most + 1) // 4
+        lax.fori_loop(0, fours, functools.partial(round_of, steps, 0, 4), 0)
+        lax.fori_loop(0, (most - 4 * fours + 1) // 2, functools.partial(round_of, steps, 4 * fours, 2), 0)
 
     if group == GROUPS - 1:
         for step in range(RING):
-            result = sums[step] / totals[step]
+            result = sums[step] * (1.0 / totals[step])
             for g in range(GROUP):
                 o_refs[step][:, g * DH : (g + 1) * DH] = (
                     result[:, g * TILE : (g + 1) * TILE].T.astype(jnp.bfloat16)
@@ -290,21 +289,23 @@
 
 def on_device(queries, keys, values, ancestry, leaf_tiles):
     table = chain_tables(ancestry, leaf_tiles)
-    sent_across, sent_first, sent_third, sent_queries = pack(queries, keys, values)
+    sent_here, sent_opposite, sent_first, sent_third, sent_queries = pack(queries, keys, values)
     block = 2 * keys.shape[0]
 
     got_first, got_third = turn(sent_first, 1), turn(sent_third, 3)
-    got_across = across(sent_across, 2)
+    got_here, got_opposite = across(sent_here, 2), across(sent_opposite, 2)
     got_queries = turn(sent_queries, 2)
-    sent_across, got_across, got_first, got_third, got_queries, table = lax.optimization_barrier(
-        (sent_across, got_across, got_first, got_third, got_queries, table)
+    got_first, got_third, got_queries, got_here, got_opposite, sent_here, sent_opposite, table = (
+        lax.optimization_barrier(
+            (got_first, got_third, got_queries, got_here, got_opposite, sent_here, sent_opposite, table)
+        )
     )
     query_parts = [queries, got_first, got_queries, got_third]
 
-    got_last = turn(jnp.concatenate([sent_across[block:], got_across[block:]], axis=0), 2)
+    got_last = turn(jnp.concatenate([sent_opposite, got_opposite], axis=0), 2)
     own_sides = jnp.concatenate([got_first[:block], got_third[:block]], axis=0)
     far_sides = across(own_sides, 2)
-    here = jnp.concatenate([sent_across[:block], got_across[:block]], axis=0)
+    here = jnp.concatenate([sent_here, got_here], axis=0)
     swapped_here, near_sides = across(here, 1), across(own_sides, 1)
     parts = [here, own_sides, swapped_here, near_sides]
     *state, query_parts[0] = attend(0, table, query_parts, parts, [], 10**8)

time: 59.5 us -> 60.2 us (1.012)
  the two profiles are of different devices: /device:TPU:2 before, /device:TPU:199 now
where the time goes in v2:
time: 60.2 us; the launch traced here: 60.1 us
  Pallas kernels  26.1 us (43%)
  waiting for transfers between devices  21.2 us (35%)
  starting transfers between devices  12.4 us (21%)
    pallas_call x3, Pallas kernels, attend(): pl.pallas_call(functools.partial(attend_kernel, group, len(kv_parts)), ou...  18.1 us
    ppermute x7, waiting for transfers between devices, turn(): lax.ppermute(array, 'kv', [(i, (i + by) % RING) for i in range(RING)])  17.5 us
    ppermute x7, starting transfers between devices, turn(): lax.ppermute(array, 'kv', [(i, (i + by) % RING) for i in range(RING)])  7.01 us
    pallas_call x1, Pallas kernels, chain_tables(): pl.pallas_call(tables_kernel, out_shape=jax.ShapeDtypeStruct((GROUPS * RI...  5.53 us
    ppermute x7, starting transfers between devices, across(): return lax.ppermute(array, 'blk', [(i, i ^ bit) for i in range(BLKS)])  5.36 us
    ppermute x7, waiting for transfers between devices, across(): return lax.ppermute(array, 'blk', [(i, i ^ bit) for i in range(BLKS)])  3.77 us
    pallas_call x1, Pallas kernels, pack(): pl.pallas_call(pack_kernel, out_shape=[pltpu.VMEM((length, DH), jnp.bfloa...  1.58 us
  transfers between devices with their start and end apart: 14, of which 8 were waited for; matrix products, arithmetic and copies ran while one was open for 0% of the time, Pallas kernels for 27%

profile of v2, /device:TPU:199, one launch (start us, length us, event | category | flops | bytes accessed | tf_op | source)
XLA Modules:
  0.0 60.1 jit_solution(17957268730409064794)
XLA Ops:
  0.0 1.6 %pack.1 = (bf16[1024,128]{1,0:T(8,128)(2,1)S(1)}, bf16[1024,128]{1,0:T(8,128)(2,1)S(1)}, bf16[1664,128]{1,0:T(8,128)(2,1)S(1)}, bf16[1664,128]{1,0:T(8,128)(2,1)S(1)}, bf16[640,128]{1,0:T(8,128)(2,1)S(1)}) custom-call(bf16[128,2560]{1,0:T(8,128)(2,1)} %refs_0_.1, bf16[512,512]{1,0:T(8,128)(2,1)} %keys_ref.1, bf16[512,512]{1,0:T(8,128)(2,1)} %values_ref.1), custom_call_target="tpu_custom_call" | custom-call | tf_op jit(solution)/shard_map/pack/pallas_call | solution.py:59
  1.6 1.4 %collective-permute-start = (bf16[1664,128]{1,0:T(8,128)(2,1)S(1)}, bf16[1664,128]{1,0:T(8,128)(2,1)S(1)}, u32[]{:S(2)}, u32[]{:S(2)}) collective-permute-start(bf16[1664,128]{1,0:T(8,128)(2,1)S(1)} %get-tuple-element.37), channel_id=1, source_target_pairs={{0,1},{1,2},{2,3},{3,0},{4,5},{5,6},{6,7},{7,4},{8,9},{9,10},{10,1... | collective-permute-start | bytes 1277960 | tf_op jit(solution)/shard_map/ppermute | solution.py:283
  3.0 1.5 %collective-permute-start.1 = (bf16[1664,128]{1,0:T(8,128)(2,1)S(1)}, bf16[1664,128]{1,0:T(8,128)(2,1)S(1)}, u32[]{:S(2)}, u32[]{:S(2)}) collective-permute-start(bf16[1664,128]{1,0:T(8,128)(2,1)S(1)} %get-tuple-element.38), channel_id=1, source_target_pairs={{0,3},{1,0},{2,1},{3,2},{4,7},{5,4},{6,5},{7,6},{8,11},{9,8},{10,9... | collective-permute-start | bytes 1277960 | tf_op jit(solution)/shard_map/ppermute | solution.py:283
  4.5 0.5 collective-permute-start.3
  5.0 0.9 %collective-permute-start.4 = (bf16[1024,128]{1,0:T(8,128)(2,1)S(1)}, bf16[1024,128]{1,0:T(8,128)(2,1)S(1)}, u32[]{:S(2)}, u32[]{:S(2)}) collective-permute-start(bf16[1024,128]{1,0:T(8,128)(2,1)S(1)} %get-tuple-element.53), channel_id=1, source_target_pairs={{0,8},{4,12},{8,0},{12,4},{1,9},{5,13},{9,1},{13,5},{2,10},{6,14},... | collective-permute-start | bytes 786440 | tf_op jit(solution)/shard_map/ppermute | solution.py:287
  6.0 1.6 %collective-permute-start.2 = (bf16[640,128]{1,0:T(8,128)(2,1)S(1)}, bf16[640,128]{1,0:T(8,128)(2,1)S(1)}, u32[]{:S(2)}, u32[]{:S(2)}) collective-permute-start(bf16[640,128]{1,0:T(8,128)(2,1)S(1)} %get-tuple-element.39), channel_id=1, source_target_pairs={{0,2},{1,3},{2,0},{3,1},{4,6},{5,7},{6,4},{7,5},{8,10},{9,11},{10,... | collective-permute-start | bytes 491528 | tf_op jit(solution)/shard_map/ppermute | solution.py:283
  7.5 5.5 %tables.1.table_ref = s32[12,40]{1,0:T(8,128)S(1)} custom-call(s32[16,64]{1,0:T(8,128)S(1)} %copy-done, s32[16]{0:T(128)S(1)} %copy-done.1), custom_call_target="tpu_custom_call" | custom-call | bytes 100000000 | tf_op jit(solution)/shard_map/tables/pallas_call | solution.py:271
  13.1 5.3 %collective-permute-done.2.refs_2_ = bf16[640,128]{1,0:T(8,128)(2,1)S(1)} collective-permute-done((bf16[640,128]{1,0:T(8,128)(2,1)S(1)}, bf16[640,128]{1,0:T(8,128)(2,1)S(1)}, u32[]{:S(2)}, u32[]{:S(2)}) %collective-permute-start.2) | collective-permute-done | bytes 163872 | tf_op jit(solution)/shard_map/ppermute | solution.py:283
  18.3 0.0 collective-permute-done.3
  18.3 0.0 collective-permute-done.4
  18.3 0.0 collective-permute-done.refs_1_
  18.4 0.6 %collective-permute-start.7 = (bf16[2048,128]{1,0:T(8,128)(2,1)S(1)}, bf16[2048,128]{1,0:T(8,128)(2,1)S(1)}, u32[]{:S(2)}, u32[]{:S(2)}) collective-permute-start(bf16[2048,128]{1,0:T(8,128)(2,1)S(1)} %pad_maximum_fusion.refs_5_), channel_id=1, source_target_pairs={{0,8},{4,12},{8,0},{12,4},{1,9},{5,13},{9,1},{13,5},{2,10},{6,14},... | collective-permute-start | bytes 1572872 | tf_op jit(solution)/shard_map/ppermute | solution.py:287
  19.1 1.8 %collective-permute-start.6 = (bf16[2048,128]{1,0:T(8,128)(2,1)S(1)}, bf16[2048,128]{1,0:T(8,128)(2,1)S(1)}, u32[]{:S(2)}, u32[]{:S(2)}) collective-permute-start(bf16[2048,128]{1,0:T(8,128)(2,1)S(1)} %pad_maximum_fusion.refs_5_), channel_id=1, source_target_pairs={{0,4},{4,0},{8,12},{12,8},{1,5},{5,1},{9,13},{13,9},{2,6},{6,2},{1... | collective-permute-start | bytes 1572872 | tf_op jit(solution)/shard_map/ppermute | solution.py:287
  21.0 0.1 collective-permute-start.5
  21.1 0.6 collective-permute-start.9
  21.7 0.7 %collective-permute-done.6.refs_7_ = bf16[2048,128]{1,0:T(8,128)(2,1)S(1)} collective-permute-done((bf16[2048,128]{1,0:T(8,128)(2,1)S(1)}, bf16[2048,128]{1,0:T(8,128)(2,1)S(1)}, u32[]{:S(2)}, u32[]{:S(2)}) %collective-permute-start.6) | collective-permute-done | bytes 524320 | tf_op jit(solution)/shard_map/ppermute | solution.py:287
  22.4 0.7 %collective-permute-done.5.refs_6_ = bf16[2048,128]{1,0:T(8,128)(2,1)S(1)} collective-permute-done((bf16[2048,128]{1,0:T(8,128)(2,1)S(1)}, bf16[2048,128]{1,0:T(8,128)(2,1)S(1)}, u32[]{:S(2)}, u32[]{:S(2)}) %collective-permute-start.5) | collective-permute-done | bytes 524320 | tf_op jit(solution)/shard_map/ppermute | solution.py:287
  23.2 7.8 %attend.3 = (f32[4,1,640]{2,1,0:T(1,128)S(1)}, f32[4,1,640]{2,1,0:T(1,128)S(1)}, f32[4,128,640]{2,1,0:T(8,128)S(1)}, bf16[640,128]{1,0:T(8,128)(2,1)S(1)}) custom-call(s32[12,40]{1,0:T(8,128)S(1)} %tables.1.table_ref, bf16[128,2560]{1,0:T(8,128)(2,1)} %refs_0_.1, bf16[1664,128]{1,0:T(8,128)(2,1)S(1)} %collective-permute-done.refs_1_, ...), custom_call_target="tpu_custom_call" | custom-call | bytes 100000000 | tf_op jit(solution)/shard_map/attend/pallas_call | solution.py:216
  31.0 2.9 %attend.4 = (f32[4,1,640]{2,1,0:T(1,128)S(1)}, f32[4,1,640]{2,1,0:T(1,128)S(1)}, f32[4,128,640]{2,1,0:T(8,128)S(1)}) custom-call(s32[12,40]{1,0:T(8,128)S(1)} %tables.1.table_ref, bf16[640,128]{1,0:T(8,128)(2,1)S(1)} %get-tuple-element.48.refs_0_, ...), custom_call_target="tpu_custom_call", output_to_operand_aliasing={{0}: (6, {}), {1}: (7, {}), {2}: (8, {})} | custom-call | bytes 10 | tf_op jit(solution)/shard_map/attend/pallas_call | solution.py:216
  33.9 1.8 %collective-permute-done.9.refs_5_ = bf16[2048,128]{1,0:T(8,128)(2,1)S(1)} collective-permute-done((bf16[2048,128]{1,0:T(8,128)(2,1)S(1)}, bf16[2048,128]{1,0:T(8,128)(2,1)S(1)}, u32[]{:S(2)}, u32[]{:S(2)}) %collective-permute-start.9) | collective-permute-done | bytes 524320 | tf_op jit(solution)/shard_map/ppermute | solution.py:283
  35.7 1.3 %collective-permute-start.10 = (bf16[2048,128]{1,0:T(8,128)(2,1)S(1)}, bf16[2048,128]{1,0:T(8,128)(2,1)S(1)}, u32[]{:S(2)}, u32[]{:S(2)}) collective-permute-start(bf16[2048,128]{1,0:T(8,128)(2,1)S(1)} %collective-permute-done.9.refs_5_), channel_id=1, source_target_pairs={{0,4},{4,0},{8,12},{12,8},{1,5},{5,1},{9,13},{13,9},{2,6},{6,2},{1... | collective-permute-start | bytes 1572872 | tf_op jit(solution)/shard_map/ppermute | solution.py:287
  37.0 0.0 collective-permute-start.8
  37.0 1.5 %collective-permute-done.10.refs_6_ = bf16[2048,128]{1,0:T(8,128)(2,1)S(1)} collective-permute-done((bf16[2048,128]{1,0:T(8,128)(2,1)S(1)}, bf16[2048,128]{1,0:T(8,128)(2,1)S(1)}, u32[]{:S(2)}, u32[]{:S(2)}) %collective-permute-start.10) | collective-permute-done | bytes 524320 | tf_op jit(solution)/shard_map/ppermute | solution.py:287
  38.6 0.7 %collective-permute-done.8.refs_4_ = bf16[2048,128]{1,0:T(8,128)(2,1)S(1)} collective-permute-done((bf16[2048,128]{1,0:T(8,128)(2,1)S(1)}, bf16[2048,128]{1,0:T(8,128)(2,1)S(1)}, u32[]{:S(2)}, u32[]{:S(2)}) %collective-permute-start.8) | collective-permute-done | bytes 524320 | tf_op jit(solution)/shard_map/ppermute | solution.py:287
  39.3 7.4 %attend.5 = (f32[4,1,640]{2,1,0:T(1,128)S(1)}, f32[4,1,640]{2,1,0:T(1,128)S(1)}, f32[4,128,640]{2,1,0:T(8,128)S(1)}, bf16[128,640]{1,0:T(8,128)(2,1)S(1)}, bf16[...) custom-call(s32[12,40]{1,0:T(8,128)S(1)} %tables.1.table_ref, ...), custom_call_target="tpu_custom_call", output_to_operand_aliasing={{0}: (8, {}), {1}: (9, {}), {2}: (10, {})} | custom-call | bytes 10 | tf_op jit(solution)/shard_map/attend/pallas_call | solution.py:216
  46.7 1.3 %collective-permute-start.11 = (bf16[128,640]{1,0:T(8,128)(2,1)S(1)}, bf16[128,640]{1,0:T(8,128)(2,1)S(1)}, u32[]{:S(2)}, u32[]{:S(2)}) collective-permute-start(bf16[128,640]{1,0:T(8,128)(2,1)S(1)} %get-tuple-element.66), channel_id=1, source_target_pairs={{0,3},{1,0},{2,1},{3,2},{4,7},{5,4},{6,5},{7,6},{8,11},{9,8},{10,9... | collective-permute-start | bytes 491528 | tf_op jit(solution)/shard_map/ppermute | solution.py:283
  48.0 0.5 collective-permute-start.12
  48.5 0.2 collective-permute-start.13
  48.6 5.4 %collective-permute-done.11.refs_1_ = bf16[128,640]{1,0:T(8,128)(2,1)S(1)} collective-permute-done((bf16[128,640]{1,0:T(8,128)(2,1)S(1)}, bf16[128,640]{1,0:T(8,128)(2,1)S(1)}, u32[]{:S(2)}, u32[]{:S(2)}) %collective-permute-start.11) | collective-permute-done | bytes 163872 | tf_op jit(solution)/shard_map/ppermute | solution.py:283
  54.1 0.0 collective-permute-done.12.refs_2_
  54.1 5.0 %collective-permute-done.13.refs_3_ = bf16[128,640]{1,0:T(8,128)(2,1)S(1)} collective-permute-done((bf16[128,640]{1,0:T(8,128)(2,1)S(1)}, bf16[128,640]{1,0:T(8,128)(2,1)S(1)}, u32[]{:S(2)}, u32[]{:S(2)}) %collective-permute-start.13) | collective-permute-done | bytes 163872 | tf_op jit(solution)/shard_map/ppermute | solution.py:283
  59.1 0.9 %unpack.1 = bf16[128,2560]{1,0:T(8,128)(2,1)} custom-call(bf16[128,640]{1,0:T(8,128)(2,1)S(1)} %get-tuple-element.65.refs_0_, bf16[128,640]{1,0:T(8,128)(2,1)S(1)} %collective-permute-done.11.refs_1_, bf16[128,640]{1,0:T(8,128)(2,1)S(1)} %collective-permute-done.12.refs_2_, bf16[128,640]{1,0:T(8,128)(2,1)S(1)} %collective-permute-done.13.refs_3_), custom_call_target="tpu_custom_call" | custom-call | tf_op jit(solution)/shard_map/unpack/pallas_call | solution.py:84
  (12 shorter events, 0.2 us)
Async XLA Ops:
  0.0 7.5 %copy-start.1 = (s32[16]{0:T(128)S(1)}, s32[16]{0:T(128)}, u32[]{:S(2)}) copy-start(s32[16]{0:T(128)} %leaf_tiles_ref.1) | copy-start | bytes 196
  0.0 7.5 %copy-start = (s32[16,64]{1,0:T(8,128)S(1)}, s32[16,64]{1,0:T(8,128)}, u32[]{:S(2)}) copy-start(s32[16,64]{1,0:T(8,128)} %ancestry_ref.1) | copy-start | bytes 12292
  1.6 16.7 %collective-permute-start = (bf16[1664,128]{1,0:T(8,128)(2,1)S(1)}, bf16[1664,128]{1,0:T(8,128)(2,1)S(1)}, u32[]{:S(2)}, u32[]{:S(2)}) collective-permute-start(bf16[1664,128]{1,0:T(8,128)(2,1)S(1)} %get-tuple-element.37), channel_id=1, source_target_pairs={{0,1},{1,2},{2,3},{3,0},{4,5},{5,6},{6,7},{7,4},{8,9},{9,10},{10,1... | collective-permute-start | bytes 1277960 | tf_op jit(solution)/shard_map/ppermute | solution.py:283
  3.0 15.4 %collective-permute-start.1 = (bf16[1664,128]{1,0:T(8,128)(2,1)S(1)}, bf16[1664,128]{1,0:T(8,128)(2,1)S(1)}, u32[]{:S(2)}, u32[]{:S(2)}) collective-permute-start(bf16[1664,128]{1,0:T(8,128)(2,1)S(1)} %get-tuple-element.38), channel_id=1, source_target_pairs={{0,3},{1,0},{2,1},{3,2},{4,7},{5,4},{6,5},{7,6},{8,11},{9,8},{10,9... | collective-permute-start | bytes 1277960 | tf_op jit(solution)/shard_map/ppermute | solution.py:283
  4.5 13.8 %collective-permute-start.3 = (bf16[1024,128]{1,0:T(8,128)(2,1)S(1)}, bf16[1024,128]{1,0:T(8,128)(2,1)S(1)}, u32[]{:S(2)}, u32[]{:S(2)}) collective-permute-start(bf16[1024,128]{1,0:T(8,128)(2,1)S(1)} %get-tuple-element.46), channel_id=1, source_target_pairs={{0,8},{4,12},{8,0},{12,4},{1,9},{5,13},{9,1},{13,5},{2,10},{6,14},... | collective-permute-start | bytes 786440 | tf_op jit(solution)/shard_map/ppermute | solution.py:287
  5.0 13.3 %collective-permute-start.4 = (bf16[1024,128]{1,0:T(8,128)(2,1)S(1)}, bf16[1024,128]{1,0:T(8,128)(2,1)S(1)}, u32[]{:S(2)}, u32[]{:S(2)}) collective-permute-start(bf16[1024,128]{1,0:T(8,128)(2,1)S(1)} %get-tuple-element.53), channel_id=1, source_target_pairs={{0,8},{4,12},{8,0},{12,4},{1,9},{5,13},{9,1},{13,5},{2,10},{6,14},... | collective-permute-start | bytes 786440 | tf_op jit(solution)/shard_map/ppermute | solution.py:287
  6.0 12.4 %collective-permute-start.2 = (bf16[640,128]{1,0:T(8,128)(2,1)S(1)}, bf16[640,128]{1,0:T(8,128)(2,1)S(1)}, u32[]{:S(2)}, u32[]{:S(2)}) collective-permute-start(bf16[640,128]{1,0:T(8,128)(2,1)S(1)} %get-tuple-element.39), channel_id=1, source_target_pairs={{0,2},{1,3},{2,0},{3,1},{4,6},{5,7},{6,4},{7,5},{8,10},{9,11},{10,... | collective-permute-start | bytes 491528 | tf_op jit(solution)/shard_map/ppermute | solution.py:283
  18.4 12.6 %collective-permute-start.7 = (bf16[2048,128]{1,0:T(8,128)(2,1)S(1)}, bf16[2048,128]{1,0:T(8,128)(2,1)S(1)}, u32[]{:S(2)}, u32[]{:S(2)}) collective-permute-start(bf16[2048,128]{1,0:T(8,128)(2,1)S(1)} %pad_maximum_fusion.refs_5_), channel_id=1, source_target_pairs={{0,8},{4,12},{8,0},{12,4},{1,9},{5,13},{9,1},{13,5},{2,10},{6,14},... | collective-permute-start | bytes 1572872 | tf_op jit(solution)/shard_map/ppermute | solution.py:287
  19.1 3.4 %collective-permute-start.6 = (bf16[2048,128]{1,0:T(8,128)(2,1)S(1)}, bf16[2048,128]{1,0:T(8,128)(2,1)S(1)}, u32[]{:S(2)}, u32[]{:S(2)}) collective-permute-start(bf16[2048,128]{1,0:T(8,128)(2,1)S(1)} %pad_maximum_fusion.refs_5_), channel_id=1, source_target_pairs={{0,4},{4,0},{8,12},{12,8},{1,5},{5,1},{9,13},{13,9},{2,6},{6,2},{1... | collective-permute-start | bytes 1572872 | tf_op jit(solution)/shard_map/ppermute | solution.py:287
  21.0 2.2 %collective-permute-start.5 = (bf16[2048,128]{1,0:T(8,128)(2,1)S(1)}, bf16[2048,128]{1,0:T(8,128)(2,1)S(1)}, u32[]{:S(2)}, u32[]{:S(2)}) collective-permute-start(bf16[2048,128]{1,0:T(8,128)(2,1)S(1)} %constant_dynamic-update-slice_fusion.refs_4_), channel_id=1, source_target_pairs={{0,4},{4,0},{8,12},{12,8},{1,5},{5,1},{9,13},{13,9},{2,6},{6,2},{1... | collective-permute-start | bytes 1572872 | tf_op jit(solution)/shard_map/ppermute | solution.py:287
  21.1 14.6 %collective-permute-start.9 = (bf16[2048,128]{1,0:T(8,128)(2,1)S(1)}, bf16[2048,128]{1,0:T(8,128)(2,1)S(1)}, u32[]{:S(2)}, u32[]{:S(2)}) collective-permute-start(bf16[2048,128]{1,0:T(8,128)(2,1)S(1)} %pad_maximum_fusion.1), channel_id=1, source_target_pairs={{0,2},{1,3},{2,0},{3,1},{4,6},{5,7},{6,4},{7,5},{8,10},{9,11},{10,... | collective-permute-start | bytes 1572872 | tf_op jit(solution)/shard_map/ppermute | solution.py:283
  35.7 2.9 %collective-permute-start.10 = (bf16[2048,128]{1,0:T(8,128)(2,1)S(1)}, bf16[2048,128]{1,0:T(8,128)(2,1)S(1)}, u32[]{:S(2)}, u32[]{:S(2)}) collective-permute-start(bf16[2048,128]{1,0:T(8,128)(2,1)S(1)} %collective-permute-done.9.refs_5_), channel_id=1, source_target_pairs={{0,4},{4,0},{8,12},{12,8},{1,5},{5,1},{9,13},{13,9},{2,6},{6,2},{1... | collective-permute-start | bytes 1572872 | tf_op jit(solution)/shard_map/ppermute | solution.py:287
  37.0 2.3 %collective-permute-start.8 = (bf16[2048,128]{1,0:T(8,128)(2,1)S(1)}, bf16[2048,128]{1,0:T(8,128)(2,1)S(1)}, u32[]{:S(2)}, u32[]{:S(2)}) collective-permute-start(bf16[2048,128]{1,0:T(8,128)(2,1)S(1)} %collective-permute-done.7.refs_4_), channel_id=1, source_target_pairs={{0,4},{4,0},{8,12},{12,8},{1,5},{5,1},{9,13},{13,9},{2,6},{6,2},{1... | collective-permute-start | bytes 1572872 | tf_op jit(solution)/shard_map/ppermute | solution.py:287
  46.7 7.4 %collective-permute-start.11 = (bf16[128,640]{1,0:T(8,128)(2,1)S(1)}, bf16[128,640]{1,0:T(8,128)(2,1)S(1)}, u32[]{:S(2)}, u32[]{:S(2)}) collective-permute-start(bf16[128,640]{1,0:T(8,128)(2,1)S(1)} %get-tuple-element.66), channel_id=1, source_target_pairs={{0,3},{1,0},{2,1},{3,2},{4,7},{5,4},{6,5},{7,6},{8,11},{9,8},{10,9... | collective-permute-start | bytes 491528 | tf_op jit(solution)/shard_map/ppermute | solution.py:283
  48.0 6.2 %collective-permute-start.12 = (bf16[128,640]{1,0:T(8,128)(2,1)S(1)}, bf16[128,640]{1,0:T(8,128)(2,1)S(1)}, u32[]{:S(2)}, u32[]{:S(2)}) collective-permute-start(bf16[128,640]{1,0:T(8,128)(2,1)S(1)} %get-tuple-element.67), channel_id=1, source_target_pairs={{0,2},{1,3},{2,0},{3,1},{4,6},{5,7},{6,4},{7,5},{8,10},{9,11},{10,... | collective-permute-start | bytes 491528 | tf_op jit(solution)/shard_map/ppermute | solution.py:283
  48.5 10.6 %collective-permute-start.13 = (bf16[128,640]{1,0:T(8,128)(2,1)S(1)}, bf16[128,640]{1,0:T(8,128)(2,1)S(1)}, u32[]{:S(2)}, u32[]{:S(2)}) collective-permute-start(bf16[128,640]{1,0:T(8,128)(2,1)S(1)} %get-tuple-element.68), channel_id=1, source_target_pairs={{0,1},{1,2},{2,3},{3,0},{4,5},{5,6},{6,7},{7,4},{8,9},{9,10},{10,1... | collective-permute-start | bytes 491528 | tf_op jit(solution)/shard_map/ppermute | solution.py:283
